TPU v7x, 32 devices: a whole 2x2x4 slice. The times are simulated.
32 devices in a mesh: dp: 4 (over z), fsdp: 4 (over y, x), tensor: 2 (over core).
Axes of the slice: x: 2, y: 2, z: 4, core: 2. Of those that a mesh axis runs over, the one named last changes fastest.
Arguments:
- activations: bfloat16 [4096, 8192], P(('dp', 'fsdp')), may hold values from -6 to 6
- out_grads: bfloat16 [4096, 2, 2048], P(('dp', 'fsdp'), 'tensor'), may hold values from -0.09375 to 0.09375
- basis: bfloat16 [8192, 1024], P('dp'), may hold values from -0.0625 to 0.0625
- weights: bfloat16 [2, 2048, 8192], P('tensor', ('dp', 'fsdp')), may hold values from -3 to 3
- first_moment: float32 [2, 2048, 1024], P('tensor', ('dp', 'fsdp')), may hold values from -2 to 2
- second_moment: float32 [2, 2048, 1024], P('tensor', ('dp', 'fsdp')), may hold values from 0.0001 to 0.01
Outputs:
- new_weights: bfloat16 [2, 2048, 8192], P('tensor', 'dp')
- first_new: float32 [2, 2048, 1024], P('tensor', ('dp', 'fsdp'))
- second_new: float32 [2, 2048, 1024], P('tensor', ('dp', 'fsdp'))
All inputs are finite; a program needn't handle non-finite values.
Results may differ from a plain program's by a relative error of at most 0.012.
Values may be sent and summed in bfloat16 or wider, within the bound.
A program may use at most 128 MiB of HBM per device.

v0:
```python
import jax
import jax.numpy as jnp
from jax import lax
from jax.sharding import PartitionSpec as P

STEP = 10


beta_one = 0.9
beta_two = 0.999
epsilon = 1e-08
step_scale = 0.25


def fold_rows(activations, shard_rows):
    running = jnp.dot(activations, shard_rows, preferred_element_type=jnp.float32)
    return (running, shard_rows)


def shards(activations, out_grads, basis, weights, first_moment, second_moment):
    cotangent = out_grads[:, 0, :]
    running, collected = fold_rows(activations, lax.all_gather(basis, "dp", axis=0, tiled=True))
    low_rank = running.astype(jnp.bfloat16)
    projected = lax.psum_scatter(
        lax.dot_general(
            cotangent, low_rank, (((0,), (0,)), ((), ())), preferred_element_type=jnp.float32
        ),
        ("dp", "fsdp"),
        scatter_dimension=0,
        tiled=True,
    )
    projected = projected[None]
    first_new = beta_one * first_moment + (1.0 - beta_one) * projected
    second_new = beta_two * second_moment + (1.0 - beta_two) * projected * projected
    corrected = first_new / (1.0 - beta_one**STEP)
    scaled = jnp.sqrt(second_new / (1.0 - beta_two**STEP)) + epsilon
    direction = (corrected / scaled).astype(jnp.bfloat16)
    update = jnp.einsum("gor,dr->god", direction, collected, preferred_element_type=jnp.float32)
    renewed = (weights.astype(jnp.float32) - step_scale * update).astype(jnp.bfloat16)
    new_weights = lax.all_gather(renewed, "fsdp", axis=1, tiled=True)
    return (new_weights, first_new, second_new)


def solution(mesh):
    return jax.shard_map(
        shards,
        mesh=mesh,
        in_specs=(
            P(("dp", "fsdp"), None),
            P(("dp", "fsdp"), "tensor", None),
            P("dp", None),
            P("tensor", ("dp", "fsdp"), None),
            P("tensor", ("dp", "fsdp"), None),
            P("tensor", ("dp", "fsdp"), None),
        ),
        out_specs=(
            P("tensor", "dp", None),
            P("tensor", ("dp", "fsdp"), None),
            P("tensor", ("dp", "fsdp"), None),
        ),
        check_vma=False,
    )
```

profile of v0, /device:TPU:0, one launch (start us, length us, event | category | flops | bytes accessed | tf_op | source)
XLA Modules:
  0.0 610.5 jit_solution(13765877406259117154)
XLA Ops:
  7.2 0.0 copy-start
  7.2 0.0 all-gather.3.cloned.1.call-start
  7.2 0.7 all-gather.3.cloned.1.call-update
  7.9 0.0 reduce-scatter.2.cloned.1.call-start
  8.0 291.1 %all-gather.3.cloned.1.call-done = bf16[8192,1024]{1,0:T(8,128)(2,1)} async-done(((bf16[2048,1024]{1,0:T(8,128)(2,1)}), bf16[8192,1024]{1,0:T(8,128)(2,1)}) %all-gather.3.cloned.1.call-update) | async-done | bytes 16777232 | tf_op jit(solution)/shard_map/all_gather | solution.py:22
  299.1 0.0 copy-done
  299.1 16.1 %convolution_bitcast_fusion = f32[2048,1024]{0,1:T(8,128)} fusion(bf16[256,8192]{1,0:T(8,128)(2,1)} %param.6, bf16[8192,1024]{1,0:T(8,128)(2,1)} %all-gather.3.cloned.1.call-done, bf16[256,1,2048]{2,0,1:T(8,128)(2,1)S(1)} %copy-done), kind=kOutput, calls=%fused_computation.4 | convolution fusion | flops 5368971264 | bytes 30408704 | tf_op jit(solution)/shard_map/dot_general | solution.py:25
  315.2 0.0 copy-start.1
  315.2 0.0 copy-start.2
  315.2 0.0 reduce-scatter.2.cloned.1.call-update
  315.2 0.0 all-gather.5.cloned.1.call-start
  315.2 1.0 copy-done.1
  316.2 0.2 copy.10
  316.4 0.0 copy-done.2
  316.4 0.2 copy.9
  316.6 174.7 %reduce-scatter.2.cloned.1.call-done = f32[128,1024]{0,1:T(8,128)} async-done(((f32[2048,1024]{0,1:T(8,128)}), f32[128,1024]{0,1:T(8,128)}) %reduce-scatter.2.cloned.1.call-update) | async-done | bytes 524304 | tf_op jit(solution)/shard_map/reduce_scatter | solution.py:24
  491.3 1.2 bitcast_add_fusion
  492.5 13.4 %fusion.2 = bf16[1,128,8192]{2,1,0:T(8,128)(2,1)} fusion(bf16[8192,1024]{1,0:T(8,128)(2,1)} %all-gather.3.cloned.1.call-done, bf16[1,128,8192]{2,1,0:T(8,128)(2,1)} %param.9, f32[1,128,1024]{1,2,0:T(8,128)S(1)} %get-tuple-element.7, f32[1,128,1024]{1,2,0:T(8,128)S(1)} %get-tuple-element.6), kind=kOutput, calls=%fused_computation.3 | convolution fusion | flops 2152333312 | bytes 22020096 | tf_op jit(solution)/shard_map/gor,dr->god/dot_general | solution.py:38
  506.0 0.0 all-gather.5.cloned.1.call-update
  506.0 1.0 copy.11
  507.0 1.0 copy.12
  508.0 88.2 %all-gather.5.cloned.1.call-done = bf16[1,512,8192]{2,1,0:T(8,128)(2,1)} async-done(((bf16[1,128,8192]{2,1,0:T(8,128)(2,1)}), bf16[1,512,8192]{2,1,0:T(8,128)(2,1)}) %all-gather.5.cloned.1.call-update) | async-done | bytes 8388624 | tf_op jit(solution)/shard_map/all_gather | solution.py:40
  596.2 7.8 %copy.14 = bf16[1,512,8192]{2,1,0:T(8,128)(2,1)} copy(bf16[1,512,8192]{2,1,0:T(8,128)(2,1)} %all-gather.5.cloned.1.call-done) | data formatting | bytes 16777216
Async XLA Ops:
  7.2 291.9 %copy-start = (bf16[256,1,2048]{2,0,1:T(8,128)(2,1)S(1)}, bf16[256,1,2048]{2,0,1:T(8,128)(2,1)}, u32[]{:S(2)}) copy-start(bf16[256,1,2048]{2,0,1:T(8,128)(2,1)} %param.7) | copy-start | bytes 3145732
  7.2 291.9 %all-gather.3.cloned.1.call-start = ((), (), s32[]{:S(2)}) async-start(), calls=%async_computation.1 | async-start | bytes 20971520 | tf_op jit(solution)/shard_map/all_gather | solution.py:22
  7.9 483.4 %reduce-scatter.2.cloned.1.call-start = ((), (), s32[]{:S(2)}) async-start(), calls=%async_computation.2 | async-start | bytes 8912896 | tf_op jit(solution)/shard_map/reduce_scatter | solution.py:24
  315.2 1.0 copy-start.1
  315.2 1.2 copy-start.2
  315.2 281.0 %all-gather.5.cloned.1.call-start = ((), (), s32[]{:S(2)}) async-start(), calls=%async_computation.3 | async-start | bytes 10485760 | tf_op jit(solution)/shard_map/all_gather | solution.py:40
Sparse Core Ops, SparseCore 0:
  9.6 289.4 all-gather.2
  315.3 175.9 reduce-scatter.1
  506.1 89.9 all-gather.4
where the time goes:
time: 611 us; the launch traced here: 610 us
  waiting for transfers between devices  555 us (91%)
  matrix products  29.5 us (5%)
  between operations  13.8 us (2%)
  local copies, waits for them, and re-layouts  11.1 us (2%)
    all_gather x1, waiting for transfers between devices, shards(): lax.all_gather(basis, 'dp', axis=0, tiled=True)  291 us
    reduce_scatter x1, waiting for transfers between devices, shards(): lax.psum_scatter(lax.dot_general(cotangent, low_rank, (((0,), (0,)), ((),...  175 us
    all_gather x1, waiting for transfers between devices, shards(): new_weights = lax.all_gather(renewed, 'fsdp', axis=1, tiled=True)  88.2 us
    dot_general x1, matrix products, shards(): lax.dot_general(cotangent, low_rank, (((0,), (0,)), ((), ())), preferred_...  16.1 us
    dot_general x1, matrix products, shards(): jnp.einsum('gor,dr->god', direction, collected, preferred_element_type=jn...  13.4 us
  transfers between devices with their start and end apart: 3, of which 3 were waited for; matrix products, arithmetic and copies ran while one was open for 0% of the time, Pallas kernels for 0%

commit v1 on v0

v1 whole, which is shorter than its diff:
```python
import functools

import jax
import jax.numpy as jnp
from jax import lax
from jax.experimental import pallas as pl
from jax.experimental.pallas import tpu as pltpu
from jax.sharding import PartitionSpec as P

STEP = 10
MESH = pl.DeviceIdType.MESH
F32 = jnp.float32
BF16 = jnp.bfloat16

beta_one = 0.9
beta_two = 0.999
epsilon = 1e-08
step_scale = 0.25

FROM_Z, FROM_A, FROM_B, HALF0_B, HALF1_A, SIB_OWN, SIB_A, SIB_B, SIB_H0, SIB_H1 = range(10)


def kernel(
    nz, act_ref, grads_ref, basis_ref, weights_ref, first_ref, second_ref,
    basis_out, weights_out, direction_out, first_out, second_out,
    act, basis, grads, low, part_out, part_in, part_own, direction, acc,
    local, send, arrive_basis, arrive_grads, arrive_low, arrive_part, arrive_dir, arrive_w,
):
    z, j, c = lax.axis_index("dp"), lax.axis_index("fsdp"), lax.axis_index("tensor")
    a = j + 1 - 2 * lax.rem(j, 2)
    b = lax.rem(j + 2, 4)
    opposite = 3 - j
    to_a, to_b, to_o = {"fsdp": a}, {"fsdp": b}, {"fsdp": opposite}
    to_sib = {"tensor": 1 - c}
    shard = basis_ref.shape[0]
    piece = shard // 8
    half = piece // 2
    tokens = act.shape[0]
    width = act.shape[1]
    owned = first_ref.shape[0]
    columns = weights_ref.shape[1]

    peers = [lax.rem(z + step, nz) for step in range(1, nz)]

    barrier = pltpu.get_barrier_semaphore()
    for target in [{"dp": peer} for peer in peers] + [to_a, to_b, to_o, to_sib]:
        pl.semaphore_signal(barrier, inc=1, device_id=target, device_id_type=MESH)
    pl.semaphore_wait(barrier, nz - 1 + 4)

    pending = []

    def push(src, dst, arrival, target):
        copy = pltpu.make_async_remote_copy(
            src_ref=src, dst_ref=dst, send_sem=send.at[len(pending)], recv_sem=arrival,
            device_id=target, device_id_type=MESH,
        )
        copy.start()
        pending.append(copy)

    def arrived(dst, arrival):
        pltpu.make_async_remote_copy(
            src_ref=dst, dst_ref=dst, send_sem=send.at[0], recv_sem=arrival,
            device_id=to_sib, device_id_type=MESH,
        ).wait_recv()

    def rows(zs, place, core, part=None):
        start = zs * shard + (place * 2 + core) * piece
        if part is None:
            return basis.at[pl.ds(pl.multiple_of(start, piece), piece)]
        return basis.at[pl.ds(pl.multiple_of(start + part * half, half), half)]

    def sem(kind, zs):
        return arrive_basis.at[kind * nz + zs]

    mine = basis_ref.at[pl.ds(pl.multiple_of((j * 2 + c) * piece, piece), piece)]
    for peer in peers:
        push(mine, rows(z, j, c), sem(FROM_Z, z), {"dp": peer})
    get_basis = pltpu.make_async_copy(
        basis_ref, basis.at[pl.ds(pl.multiple_of(z * shard, shard), shard)], local.at[0])
    get_act = pltpu.make_async_copy(
        act_ref.at[pl.ds(pl.multiple_of(c * tokens, tokens), tokens)], act, local.at[1])
    get_weights = pltpu.make_async_copy(weights_ref, weights_out.at[j], local.at[2])
    get_grads = pltpu.make_async_copy(grads_ref.at[j], grads.at[j], local.at[3])
    for copy in (get_basis, get_act, get_grads, get_weights):
        copy.start()
    for n, (place, target) in enumerate(((a, to_a), (b, to_b), (opposite, to_o))):
        push(grads_ref.at[place], grads.at[j], arrive_grads.at[n], target)

    def w_half(ref, part):
        return ref.at[:, pl.ds(part * (columns // 2), columns // 2)]

    def send_weights(part):
        push(w_half(weights_ref, part), w_half(weights_out.at[j], part), arrive_w.at[2 * part], to_a)
        push(w_half(weights_ref, part), w_half(weights_out.at[j], part), arrive_w.at[2 * part + 1], to_b)

    send_weights(0)

    def source(k):
        near = jnp.where(z < nz // 2, z, nz - 1 - z)
        s = jnp.where(k < near, k, k + 1)
        return jnp.where(z < nz // 2, s, nz - 1 - s)

    def forward(zs):
        arrived(rows(zs, a, c), sem(FROM_A, zs))
        push(rows(zs, a, c, 0), rows(zs, a, c, 0), sem(HALF0_B, zs), to_b)
        push(rows(zs, a, c), rows(zs, a, c), sem(SIB_A, zs), to_sib)
        arrived(rows(zs, b, c), sem(FROM_B, zs))
        push(rows(zs, b, c, 1), rows(zs, b, c, 1), sem(HALF1_A, zs), to_a)
        push(rows(zs, b, c), rows(zs, b, c), sem(SIB_B, zs), to_sib)

    def finish(zs):
        arrived(rows(zs, opposite, c, 0), sem(HALF0_B, zs))
        push(rows(zs, opposite, c, 0), rows(zs, opposite, c, 0), sem(SIB_H0, zs), to_sib)
        arrived(rows(zs, opposite, c, 1), sem(HALF1_A, zs))
        push(rows(zs, opposite, c, 1), rows(zs, opposite, c, 1), sem(SIB_H1, zs), to_sib)

    for k in range(nz - 1):
        zs = source(k)
        arrived(rows(zs, j, c), sem(FROM_Z, zs))
        push(rows(zs, j, c), rows(zs, j, c), sem(FROM_A, zs), to_a)
        push(rows(zs, j, c), rows(zs, j, c), sem(FROM_B, zs), to_b)
        push(rows(zs, j, c), rows(zs, j, c), sem(SIB_OWN, zs), to_sib)
        if k >= 1:
            forward(source(k - 1))
        if k >= 2:
            finish(source(k - 2))
    forward(source(nz - 2))
    if nz >= 3:
        finish(source(nz - 3))
    finish(source(nz - 2))

    arrived(w_half(weights_out.at[a], 0), arrive_w.at[0])
    push(w_half(weights_out.at[a], 0), w_half(weights_out.at[a], 0), arrive_w.at[4], to_b)

    for k in range(nz - 1):
        zs = source(k)
        arrived(rows(zs, j, 1 - c), sem(SIB_OWN, zs))
        arrived(rows(zs, a, 1 - c), sem(SIB_A, zs))
        arrived(rows(zs, b, 1 - c), sem(SIB_B, zs))
        arrived(rows(zs, opposite, 1 - c, 0), sem(SIB_H0, zs))
        arrived(rows(zs, opposite, 1 - c, 1), sem(SIB_H1, zs))
    get_basis.wait()
    get_act.wait()

    acc[...] = jnp.zeros_like(acc)
    depth = 512

    @pl.loop(0, width // depth)
    def _(k):
        at = pl.ds(pl.multiple_of(k * depth, depth), depth)
        acc[...] += jnp.dot(act[:, at], basis[at, :], preferred_element_type=F32)

    def low_rows(place, core):
        return low.at[place, pl.ds(pl.multiple_of(core * tokens, tokens), tokens)]

    low[j, pl.ds(pl.multiple_of(c * tokens, tokens), tokens), :] = acc[...].astype(BF16)
    for n, target in enumerate((to_a, to_b, to_o, to_sib)):
        push(low_rows(j, c), low_rows(j, c), arrive_low.at[n], target)
    put_basis = pltpu.make_async_copy(basis, basis_out, local.at[4])
    put_basis.start()
    send_weights(1)
    for n, place in enumerate((a, b, opposite)):
        arrived(low_rows(place, c), arrive_low.at[n])
        push(low_rows(place, c), low_rows(place, c), arrive_low.at[4 + n], to_sib)
    for n, place in ((3, j), (4, a), (5, b), (6, opposite)):
        arrived(low_rows(place, 1 - c), arrive_low.at[n])
    for n, place in enumerate((a, b, opposite)):
        arrived(grads.at[place], arrive_grads.at[n])
    get_grads.wait()

    def partial(peer):
        at = pl.ds(pl.multiple_of(peer * owned, owned), owned)
        total = jnp.dot(grads[0, at, :], low[0], preferred_element_type=F32)
        for place in range(1, 4):
            total += jnp.dot(grads[place, at, :], low[place], preferred_element_type=F32)
        return total

    @pl.loop(1, nz)
    def _(step):
        peer = lax.rem(z + step, nz)
        part_out[peer] = partial(peer).astype(BF16)

    for peer in peers:
        push(part_out.at[peer], part_in.at[z], arrive_part.at[z], {"dp": peer})
    part_own[...] = partial(z)

    for peer in peers:
        arrived(part_in.at[peer], arrive_part.at[peer])
        part_own[...] += part_in[peer].astype(F32)

    projected = part_own[...]
    first_new = beta_one * first_ref[...] + (1.0 - beta_one) * projected
    second_new = beta_two * second_ref[...] + (1.0 - beta_two) * projected * projected
    first_out[...] = first_new
    second_out[...] = second_new
    corrected = first_new / (1.0 - beta_one**STEP)
    scaled = jnp.sqrt(second_new / (1.0 - beta_two**STEP)) + epsilon
    direction[j] = (corrected / scaled).astype(BF16)
    for n, target in enumerate((to_a, to_b, to_o)):
        push(direction.at[j], direction.at[j], arrive_dir.at[n], target)

    arrived(w_half(weights_out.at[b], 1), arrive_w.at[3])
    push(w_half(weights_out.at[b], 1), w_half(weights_out.at[b], 1), arrive_w.at[5], to_a)
    for n, place in enumerate((a, b, opposite)):
        arrived(direction.at[place], arrive_dir.at[n])
    put_direction = pltpu.make_async_copy(direction, direction_out, local.at[5])
    put_direction.start()
    arrived(w_half(weights_out.at[b], 0), arrive_w.at[1])
    arrived(w_half(weights_out.at[a], 1), arrive_w.at[2])
    arrived(w_half(weights_out.at[opposite], 0), arrive_w.at[4])
    arrived(w_half(weights_out.at[opposite], 1), arrive_w.at[5])
    get_weights.wait()
    put_basis.wait()
    put_direction.wait()
    for copy in pending:
        copy.wait_send()


def shards(nz, activations, out_grads, basis, weights, first_moment, second_moment):
    tokens, width = activations.shape
    shard, rank = basis.shape
    owned = first_moment.shape[1]
    features = 4 * owned
    grads = out_grads[:, 0, :].reshape(tokens, nz, 4, owned)
    grads = grads.transpose(2, 1, 3, 0).reshape(4, nz * owned, tokens)
    vmem = pl.BlockSpec(memory_space=pltpu.VMEM)
    hbm = pl.BlockSpec(memory_space=pl.ANY)
    dma = pltpu.SemaphoreType.DMA
    sends = (nz - 1) * 11 + (nz - 1) + 3 + 6 + 7 + 3
    gathered, weight_rows, direction, first_new, second_new = pl.pallas_call(
        functools.partial(kernel, nz),
        out_shape=(
            jax.ShapeDtypeStruct((nz * shard, rank), BF16),
            jax.ShapeDtypeStruct((4, owned, width), BF16),
            jax.ShapeDtypeStruct((4, owned, rank), BF16),
            jax.ShapeDtypeStruct((owned, rank), F32),
            jax.ShapeDtypeStruct((owned, rank), F32),
        ),
        in_specs=[hbm, hbm, hbm, hbm, vmem, vmem],
        out_specs=(hbm, hbm, hbm, vmem, vmem),
        scratch_shapes=[
            pltpu.VMEM((tokens // 2, width), BF16),
            pltpu.VMEM((nz * shard, rank), BF16),
            pltpu.VMEM((4, nz * owned, tokens), BF16),
            pltpu.VMEM((4, tokens, rank), BF16),
            pltpu.VMEM((nz, owned, rank), BF16),
            pltpu.VMEM((nz, owned, rank), BF16),
            pltpu.VMEM((owned, rank), F32),
            pltpu.VMEM((4, owned, rank), BF16),
            pltpu.VMEM((tokens // 2, rank), F32),
            dma((6,)),
            dma((sends,)),
            dma((10 * nz,)),
            dma((3,)),
            dma((7,)),
            dma((nz,)),
            dma((3,)),
            dma((6,)),
        ],
        compiler_params=pltpu.CompilerParams(
            collective_id=0, has_side_effects=True, vmem_limit_bytes=50 * 2**20
        ),
        name="gather_and_step",
    )(activations, grads, basis, weights[0], first_moment[0], second_moment[0])
    update = lax.dot_general(
        direction.reshape(features, rank), gathered, (((1,), (1,)), ((), ())),
        preferred_element_type=F32,
    )
    rows = weight_rows.reshape(features, width)
    new_weights = (rows.astype(F32) - step_scale * update).astype(BF16)
    return (new_weights[None], first_new[None], second_new[None])


def solution(mesh):
    return jax.shard_map(
        functools.partial(shards, mesh.shape["dp"]),
        mesh=mesh,
        in_specs=(
            P(("dp", "fsdp"), None),
            P(("dp", "fsdp"), "tensor", None),
            P("dp", None),
            P("tensor", ("dp", "fsdp"), None),
            P("tensor", ("dp", "fsdp"), None),
            P("tensor", ("dp", "fsdp"), None),
        ),
        out_specs=(
            P("tensor", "dp", None),
            P("tensor", ("dp", "fsdp"), None),
            P("tensor", ("dp", "fsdp"), None),
        ),
        check_vma=False,
    )
```

time: 611 us -> 214 us (0.35)
  waiting for transfers between devices: 555 us -> 0 us
  Pallas kernels: 0 us -> 187 us
  matrix products: 29.5 us -> 15.7 us
  between operations: 13.8 us -> 0.65 us
    all_gather x2 -> x0, waiting for transfers between devices: 379 us -> none  [the longest x1 291 us: shards(): lax.all_gather(basis, 'dp', axis=0, tiled=True)]
    pallas_call x0 -> x1, Pallas kernels: none -> 187 us  [shards(): pl.pallas_call(functools.partial(kernel, nz), out_shape=(jax.ShapeDtypeSt...]
    reduce_scatter x1 -> x0, waiting for transfers between devices: 175 us -> none  [shards(): lax.psum_scatter(lax.dot_general(cotangent, low_rank, (((0,), (0,)), ((),...]
    dot_general x2 -> x1, matrix products: 29.5 us -> 15.7 us  [shards(): lax.dot_general(direction.reshape(features, rank), gathered, (((1,), (1,)...]
    unnamed x11 -> x6, local copies, waits for them, and re-layouts: 11.1 us -> 3.67 us
  transfers between devices with their start and end apart: 3 -> 0, of which waited for: 3 -> 0; matrix products, arithmetic and copies ran while one was open for 0% -> 0% of each run, Pallas kernels for 0% -> 0%
where the time goes in v1:
time: 214 us; the launch traced here: 210 us
  Pallas kernels  187 us (87%)
  matrix products  15.7 us (7%)
  local copies, waits for them, and re-layouts  7.02 us (3%)
    pallas_call x1, Pallas kernels, shards(): pl.pallas_call(functools.partial(kernel, nz), out_shape=(jax.ShapeDtypeSt...  187 us
    dot_general x1, matrix products, shards(): lax.dot_general(direction.reshape(features, rank), gathered, (((1,), (1,)...  15.7 us

profile of v1, /device:TPU:0, one launch (start us, length us, event | category | flops | bytes accessed | tf_op | source)
XLA Modules:
  0.0 210.1 jit_solution(12083029290797166716)
XLA Ops:
  0.6 1.8 reshape_squeeze.3
  2.4 1.6 copy.9
  4.0 0.0 copy-start
  4.0 1.0 copy-done
  5.0 0.0 copy-start.1
  5.0 1.0 copy-done.1
  6.1 186.7 %gather_and_step.1 = (bf16[8192,1024]{1,0:T(8,128)(2,1)}, bf16[4,128,8192]{2,1,0:T(8,128)(2,1)}, bf16[4,128,1024]{2,1,0:T(8,128)(2,1)S(1)}, f32[128,1024]{1,0:T(8,128)S(1)}, f32[128,1024]{1,0:T(8,128)S(1)}) custom-call(bf16[256,8192]{1,0:T(8,128)(2,1)} %act_ref.1, bf16[4,512,256]{2,1,0:T(8,128)(2,1)} %bitcast.22, bf16[2048,1024]{1,0:T(8,128)(2,1)} %basis_ref.1, ...), custom_call_target="tpu_custom_call" | custom-call | tf_op jit(solution)/shard_map/gather_and_step/pallas_call | solution.py:230
  192.8 15.7 %fusion.1 = bf16[1,512,8192]{2,1,0:T(8,128)(2,1)} fusion(bf16[512,1024]{1,0:T(8,128)(2,1)S(1)} %bitcast.21, bf16[8192,1024]{1,0:T(8,128)(2,1)} %get-tuple-element.10, bf16[512,8192]{1,0:T(8,128)(2,1)} %bitcast.24), kind=kOutput, calls=%fused_computation.2 | convolution fusion | flops 8606711808 | bytes 34603008 | tf_op jit(solution)/shard_map/dot_general | solution.py:265
  208.5 0.8 copy.12
  209.3 0.8 copy.13
Async XLA Ops:
  4.0 1.0 copy-start
  5.0 1.0 copy-start.1

commit v2 on v1

--- a/solution.py
+++ b/solution.py
@@ -23,8 +23,8 @@
 def kernel(
     nz, act_ref, grads_ref, basis_ref, weights_ref, first_ref, second_ref,
     basis_out, weights_out, direction_out, first_out, second_out,
-    act, basis, grads, low, part_out, part_in, part_own, direction, acc,
-    local, send, arrive_basis, arrive_grads, arrive_low, arrive_part, arrive_dir, arrive_w,
+    act, basis, raw, turned, grads, low, part_out, part_in, part_own, direction, acc, first, second,
+    local, hop, send, arrive_basis, arrive_grads, arrive_low, arrive_part, arrive_dir, arrive_w,
 ):
     z, j, c = lax.axis_index("dp"), lax.axis_index("fsdp"), lax.axis_index("tensor")
     a = j + 1 - 2 * lax.rem(j, 2)
@@ -63,6 +63,17 @@
             device_id=to_sib, device_id_type=MESH,
         ).wait_recv()
 
+    hops = []
+
+    def relay(n, src, zs, target):
+        inside = jnp.logical_and(target >= 0, target < nz)
+        copy = pltpu.make_async_remote_copy(
+            src_ref=src, dst_ref=rows(zs, j, c), send_sem=hop.at[n], recv_sem=sem(FROM_Z, zs),
+            device_id={"dp": lax.rem(target + nz, nz)}, device_id_type=MESH,
+        )
+        pl.when(inside)(copy.start)
+        hops.append((inside, copy))
+
     def rows(zs, place, core, part=None):
         start = zs * shard + (place * 2 + core) * piece
         if part is None:
@@ -73,27 +84,45 @@
         return arrive_basis.at[kind * nz + zs]
 
     mine = basis_ref.at[pl.ds(pl.multiple_of((j * 2 + c) * piece, piece), piece)]
-    for peer in peers:
-        push(mine, rows(z, j, c), sem(FROM_Z, z), {"dp": peer})
+    relay(0, mine, z, z + 1)
+    relay(1, mine, z, z - 1)
     get_basis = pltpu.make_async_copy(
         basis_ref, basis.at[pl.ds(pl.multiple_of(z * shard, shard), shard)], local.at[0])
     get_act = pltpu.make_async_copy(
         act_ref.at[pl.ds(pl.multiple_of(c * tokens, tokens), tokens)], act, local.at[1])
     get_weights = pltpu.make_async_copy(weights_ref, weights_out.at[j], local.at[2])
-    get_grads = pltpu.make_async_copy(grads_ref.at[j], grads.at[j], local.at[3])
-    for copy in (get_basis, get_act, get_grads, get_weights):
+    get_raw = pltpu.make_async_copy(grads_ref, raw, local.at[3])
+    get_first = pltpu.make_async_copy(first_ref, first, local.at[6])
+    get_second = pltpu.make_async_copy(second_ref, second, local.at[7])
+    for copy in (get_raw, get_basis, get_act, get_weights, get_first, get_second):
         copy.start()
+
+    get_raw.wait()
+    for place in range(4):
+        for zs in range(nz):
+            begin = (zs * 4 + place) * owned
+            turned[place, zs * owned : (zs + 1) * owned, :] = raw[:, begin : begin + owned].T
     for n, (place, target) in enumerate(((a, to_a), (b, to_b), (opposite, to_o))):
-        push(grads_ref.at[place], grads.at[j], arrive_grads.at[n], target)
-
-    def w_half(ref, part):
-        return ref.at[:, pl.ds(part * (columns // 2), columns // 2)]
-
-    def send_weights(part):
-        push(w_half(weights_ref, part), w_half(weights_out.at[j], part), arrive_w.at[2 * part], to_a)
-        push(w_half(weights_ref, part), w_half(weights_out.at[j], part), arrive_w.at[2 * part + 1], to_b)
-
-    send_weights(0)
+        push(turned.at[place], grads.at[j], arrive_grads.at[n], target)
+    grads[j] = turned[j]
+
+    def chunk(ref, n):
+        return ref.at[:, pl.ds(n * (columns // 4), columns // 4)]
+
+    def send_weights(n):
+        push(chunk(weights_ref, n), chunk(weights_out.at[j], n), arrive_w.at[3 * n], to_a)
+        push(chunk(weights_ref, n), chunk(weights_out.at[j], n), arrive_w.at[3 * n + 1], to_b)
+
+    def forward_weights(n):
+        came, way, target = (a, 0, to_b) if n % 2 == 0 else (b, 1, to_a)
+        block = chunk(weights_out.at[came], n)
+        arrived(block, arrive_w.at[3 * n + way])
+        push(block, block, arrive_w.at[3 * n + 2], target)
+
+    def finish_weights(n):
+        came, way = (b, 1) if n % 2 == 0 else (a, 0)
+        arrived(chunk(weights_out.at[came], n), arrive_w.at[3 * n + way])
+        arrived(chunk(weights_out.at[opposite], n), arrive_w.at[3 * n + 2])
 
     def source(k):
         near = jnp.where(z < nz // 2, z, nz - 1 - z)
@@ -114,41 +143,43 @@
         arrived(rows(zs, opposite, c, 1), sem(HALF1_A, zs))
         push(rows(zs, opposite, c, 1), rows(zs, opposite, c, 1), sem(SIB_H1, zs), to_sib)
 
-    for k in range(nz - 1):
-        zs = source(k)
-        arrived(rows(zs, j, c), sem(FROM_Z, zs))
-        push(rows(zs, j, c), rows(zs, j, c), sem(FROM_A, zs), to_a)
-        push(rows(zs, j, c), rows(zs, j, c), sem(FROM_B, zs), to_b)
-        push(rows(zs, j, c), rows(zs, j, c), sem(SIB_OWN, zs), to_sib)
-        if k >= 1:
-            forward(source(k - 1))
-        if k >= 2:
-            finish(source(k - 2))
-    forward(source(nz - 2))
-    if nz >= 3:
-        finish(source(nz - 3))
-    finish(source(nz - 2))
-
-    arrived(w_half(weights_out.at[a], 0), arrive_w.at[0])
-    push(w_half(weights_out.at[a], 0), w_half(weights_out.at[a], 0), arrive_w.at[4], to_b)
-
-    for k in range(nz - 1):
-        zs = source(k)
+    def collect(zs):
         arrived(rows(zs, j, 1 - c), sem(SIB_OWN, zs))
         arrived(rows(zs, a, 1 - c), sem(SIB_A, zs))
         arrived(rows(zs, b, 1 - c), sem(SIB_B, zs))
         arrived(rows(zs, opposite, 1 - c, 0), sem(SIB_H0, zs))
         arrived(rows(zs, opposite, 1 - c, 1), sem(SIB_H1, zs))
+
+    depth = min(512, shard)
+
+    def accumulate(zs):
+        @pl.loop(0, shard // depth)
+        def _(k):
+            at = pl.ds(pl.multiple_of(zs * shard + k * depth, depth), depth)
+            acc[...] += jnp.dot(act[:, at], basis[at, :], preferred_element_type=F32)
+
+    for k in range(nz - 1):
+        zs = source(k)
+        arrived(rows(zs, j, c), sem(FROM_Z, zs))
+        relay(2 + k, rows(zs, j, c), zs, jnp.where(zs < z, z + 1, z - 1))
+        push(rows(zs, j, c), rows(zs, j, c), sem(FROM_A, zs), to_a)
+        push(rows(zs, j, c), rows(zs, j, c), sem(FROM_B, zs), to_b)
+        push(rows(zs, j, c), rows(zs, j, c), sem(SIB_OWN, zs), to_sib)
+    for k in range(nz - 1):
+        forward(source(k))
+    send_weights(0)
+    send_weights(1)
     get_basis.wait()
     get_act.wait()
-
     acc[...] = jnp.zeros_like(acc)
-    depth = 512
-
-    @pl.loop(0, width // depth)
-    def _(k):
-        at = pl.ds(pl.multiple_of(k * depth, depth), depth)
-        acc[...] += jnp.dot(act[:, at], basis[at, :], preferred_element_type=F32)
+    accumulate(z)
+    finish(source(0))
+    for k in range(1, nz - 1):
+        finish(source(k))
+        collect(source(k - 1))
+        accumulate(source(k - 1))
+    collect(source(nz - 2))
+    accumulate(source(nz - 2))
 
     def low_rows(place, core):
         return low.at[place, pl.ds(pl.multiple_of(core * tokens, tokens), tokens)]
@@ -158,7 +189,6 @@
         push(low_rows(j, c), low_rows(j, c), arrive_low.at[n], target)
     put_basis = pltpu.make_async_copy(basis, basis_out, local.at[4])
     put_basis.start()
-    send_weights(1)
     for n, place in enumerate((a, b, opposite)):
         arrived(low_rows(place, c), arrive_low.at[n])
         push(low_rows(place, c), low_rows(place, c), arrive_low.at[4 + n], to_sib)
@@ -166,7 +196,10 @@
         arrived(low_rows(place, 1 - c), arrive_low.at[n])
     for n, place in enumerate((a, b, opposite)):
         arrived(grads.at[place], arrive_grads.at[n])
-    get_grads.wait()
+    forward_weights(0)
+    forward_weights(1)
+    send_weights(2)
+    send_weights(3)
 
     def partial(peer):
         at = pl.ds(pl.multiple_of(peer * owned, owned), owned)
@@ -188,9 +221,11 @@
         arrived(part_in.at[peer], arrive_part.at[peer])
         part_own[...] += part_in[peer].astype(F32)
 
+    get_first.wait()
+    get_second.wait()
     projected = part_own[...]
-    first_new = beta_one * first_ref[...] + (1.0 - beta_one) * projected
-    second_new = beta_two * second_ref[...] + (1.0 - beta_two) * projected * projected
+    first_new = beta_one * first[...] + (1.0 - beta_one) * projected
+    second_new = beta_two * second[...] + (1.0 - beta_two) * projected * projected
     first_out[...] = first_new
     second_out[...] = second_new
     corrected = first_new / (1.0 - beta_one**STEP)
@@ -199,21 +234,28 @@
     for n, target in enumerate((to_a, to_b, to_o)):
         push(direction.at[j], direction.at[j], arrive_dir.at[n], target)
 
-    arrived(w_half(weights_out.at[b], 1), arrive_w.at[3])
-    push(w_half(weights_out.at[b], 1), w_half(weights_out.at[b], 1), arrive_w.at[5], to_a)
+    forward_weights(2)
+    forward_weights(3)
     for n, place in enumerate((a, b, opposite)):
         arrived(direction.at[place], arrive_dir.at[n])
     put_direction = pltpu.make_async_copy(direction, direction_out, local.at[5])
     put_direction.start()
-    arrived(w_half(weights_out.at[b], 0), arrive_w.at[1])
-    arrived(w_half(weights_out.at[a], 1), arrive_w.at[2])
-    arrived(w_half(weights_out.at[opposite], 0), arrive_w.at[4])
-    arrived(w_half(weights_out.at[opposite], 1), arrive_w.at[5])
+    for n in range(4):
+        finish_weights(n)
     get_weights.wait()
     put_basis.wait()
     put_direction.wait()
     for copy in pending:
         copy.wait_send()
+    for inside, copy in hops:
+        pl.when(inside)(copy.wait_send)
+
+
+def renew(direction_ref, basis_ref, weights_ref, out_ref):
+    update = lax.dot_general(
+        direction_ref[...], basis_ref[...], (((1,), (1,)), ((), ())), preferred_element_type=F32
+    )
+    out_ref[...] = (weights_ref[...].astype(F32) - step_scale * update).astype(BF16)
 
 
 def shards(nz, activations, out_grads, basis, weights, first_moment, second_moment):
@@ -221,12 +263,10 @@
     shard, rank = basis.shape
     owned = first_moment.shape[1]
     features = 4 * owned
-    grads = out_grads[:, 0, :].reshape(tokens, nz, 4, owned)
-    grads = grads.transpose(2, 1, 3, 0).reshape(4, nz * owned, tokens)
     vmem = pl.BlockSpec(memory_space=pltpu.VMEM)
     hbm = pl.BlockSpec(memory_space=pl.ANY)
     dma = pltpu.SemaphoreType.DMA
-    sends = (nz - 1) * 11 + (nz - 1) + 3 + 6 + 7 + 3
+    sends = (nz - 1) * 9 + (nz - 1) + 3 + 12 + 7 + 3
     gathered, weight_rows, direction, first_new, second_new = pl.pallas_call(
         functools.partial(kernel, nz),
         out_shape=(
@@ -236,11 +276,13 @@
             jax.ShapeDtypeStruct((owned, rank), F32),
             jax.ShapeDtypeStruct((owned, rank), F32),
         ),
-        in_specs=[hbm, hbm, hbm, hbm, vmem, vmem],
+        in_specs=[hbm] * 6,
         out_specs=(hbm, hbm, hbm, vmem, vmem),
         scratch_shapes=[
             pltpu.VMEM((tokens // 2, width), BF16),
             pltpu.VMEM((nz * shard, rank), BF16),
+            pltpu.VMEM((tokens, 4 * nz * owned), BF16),
+            pltpu.VMEM((4, nz * owned, tokens), BF16),
             pltpu.VMEM((4, nz * owned, tokens), BF16),
             pltpu.VMEM((4, tokens, rank), BF16),
             pltpu.VMEM((nz, owned, rank), BF16),
@@ -248,26 +290,37 @@
             pltpu.VMEM((owned, rank), F32),
             pltpu.VMEM((4, owned, rank), BF16),
             pltpu.VMEM((tokens // 2, rank), F32),
-            dma((6,)),
+            pltpu.VMEM((owned, rank), F32),
+            pltpu.VMEM((owned, rank), F32),
+            dma((8,)),
+            dma((nz + 1,)),
             dma((sends,)),
             dma((10 * nz,)),
             dma((3,)),
             dma((7,)),
             dma((nz,)),
             dma((3,)),
-            dma((6,)),
+            dma((12,)),
         ],
         compiler_params=pltpu.CompilerParams(
-            collective_id=0, has_side_effects=True, vmem_limit_bytes=50 * 2**20
+            collective_id=0, has_side_effects=True, vmem_limit_bytes=60 * 2**20
         ),
         name="gather_and_step",
-    )(activations, grads, basis, weights[0], first_moment[0], second_moment[0])
-    update = lax.dot_general(
-        direction.reshape(features, rank), gathered, (((1,), (1,)), ((), ())),
-        preferred_element_type=F32,
-    )
-    rows = weight_rows.reshape(features, width)
-    new_weights = (rows.astype(F32) - step_scale * update).astype(BF16)
+    )(activations, out_grads[:, 0, :], basis, weights[0], first_moment[0], second_moment[0])
+    block = 1024
+    new_weights = pl.pallas_call(
+        renew,
+        out_shape=jax.ShapeDtypeStruct((features, width), BF16),
+        grid=(width // block,),
+        in_specs=[
+            pl.BlockSpec((features, rank), lambda i: (0, 0)),
+            pl.BlockSpec((block, rank), lambda i: (i, 0)),
+            pl.BlockSpec((features, block), lambda i: (0, i)),
+        ],
+        out_specs=pl.BlockSpec((features, block), lambda i: (0, i)),
+        compiler_params=pltpu.CompilerParams(vmem_limit_bytes=60 * 2**20),
+        name="renew",
+    )(direction.reshape(features, rank), gathered, weight_rows.reshape(features, width))
     return (new_weights[None], first_new[None], second_new[None])
 
 

time: 214 us -> 185 us (0.86); the launches traced: 210 us -> 185 us
  matrix products: 15.7 us -> 0 us
  local copies, waits for them, and re-layouts: 7.02 us -> 1.59 us
  Pallas kernels: 187 us -> 183 us
    pallas_call x1, Pallas kernels: 187 us -> 165 us  [shards(): pl.pallas_call(functools.partial(kernel, nz), out_shape=(jax.ShapeDtypeSt...]
    pallas_call x0 -> x1, Pallas kernels: none -> 17.7 us  [shards(): pl.pallas_call(renew, out_shape=jax.ShapeDtypeStruct((features, width), B...]
    dot_general x1 -> x0, matrix products: 15.7 us -> none  [shards(): lax.dot_general(direction.reshape(features, rank), gathered, (((1,), (1,)...]
    another operation x2 -> x0, local copies, waits for them, and re-layouts: 3.36 us -> none  [shards(): grads = out_grads[:, 0, :].reshape(tokens, nz, 4, owned)]
where the time goes in v2:
time: 185 us
  Pallas kernels  183 us (99%)
    pallas_call x1, Pallas kernels, shards(): pl.pallas_call(functools.partial(kernel, nz), out_shape=(jax.ShapeDtypeSt...  165 us
    pallas_call x1, Pallas kernels, shards(): pl.pallas_call(renew, out_shape=jax.ShapeDtypeStruct((features, width), B...  17.7 us

profile of v2, /device:TPU:0, one launch (start us, length us, event | category | flops | bytes accessed | tf_op | source)
XLA Modules:
  0.0 185.0 jit_solution(14213783006936163522)
XLA Ops:
  0.6 165.1 %gather_and_step.1 = (bf16[8192,1024]{1,0:T(8,128)(2,1)}, bf16[4,128,8192]{2,1,0:T(8,128)(2,1)}, bf16[4,128,1024]{2,1,0:T(8,128)(2,1)}, f32[128,1024]{1,0:T(8,128)}, f32[128,1024]{1,0:T(8,128)}) custom-call(bf16[256,8192]{1,0:T(8,128)(2,1)} %act_ref.1, bf16[256,2048]{1,0:T(8,128)(2,1)} %bitcast.12, bf16[2048,1024]{1,0:T(8,128)(2,1)} %basis_ref.1, ...), custom_call_target="tpu_custom_call" | custom-call | tf_op jit(solution)/shard_map/gather_and_step/pallas_call | solution.py:270
  165.7 0.0 copy-start.1
  165.7 0.0 copy-start
  165.8 17.7 %renew.1 = bf16[512,8192]{1,0:T(8,128)(2,1)} custom-call(bf16[512,1024]{1,0:T(8,128)(2,1)} %bitcast.13, bf16[8192,1024]{1,0:T(8,128)(2,1)} %get-tuple-element.9.basis_ref, bf16[512,8192]{1,0:T(8,128)(2,1)} %bitcast.10), custom_call_target="tpu_custom_call" | custom-call | tf_op jit(solution)/shard_map/renew/pallas_call | solution.py:311
  183.4 0.0 copy-done.1
  183.4 0.8 copy.11
  184.2 0.0 copy-done
  184.2 0.8 copy.12
Async XLA Ops:
  165.7 17.7 %copy-start.1 = (f32[128,1024]{1,0:T(8,128)S(1)}, f32[128,1024]{1,0:T(8,128)}, u32[]{:S(2)}) copy-start(f32[128,1024]{1,0:T(8,128)} %get-tuple-element.11) | copy-start | bytes 1572868
  165.7 18.5 %copy-start = (f32[128,1024]{1,0:T(8,128)S(1)}, f32[128,1024]{1,0:T(8,128)}, u32[]{:S(2)}) copy-start(f32[128,1024]{1,0:T(8,128)} %get-tuple-element.12) | copy-start | bytes 1572868

commit v3 on v2

--- a/solution.py
+++ b/solution.py
@@ -17,7 +17,7 @@
 epsilon = 1e-08
 step_scale = 0.25
 
-FROM_Z, FROM_A, FROM_B, HALF0_B, HALF1_A, SIB_OWN, SIB_A, SIB_B, SIB_H0, SIB_H1 = range(10)
+FROM_Z, FROM_Z2, FROM_A, FROM_B, SIB_OWN, SIB_A, SIB_B, SIB_O = range(8)
 
 
 def kernel(
@@ -34,7 +34,6 @@
     to_sib = {"tensor": 1 - c}
     shard = basis_ref.shape[0]
     piece = shard // 8
-    half = piece // 2
     tokens = act.shape[0]
     width = act.shape[1]
     owned = first_ref.shape[0]
@@ -65,27 +64,28 @@
 
     hops = []
 
-    def relay(n, src, zs, target):
+    def relay(src, zs, place, kind, target):
         inside = jnp.logical_and(target >= 0, target < nz)
         copy = pltpu.make_async_remote_copy(
-            src_ref=src, dst_ref=rows(zs, j, c), send_sem=hop.at[n], recv_sem=sem(FROM_Z, zs),
-            device_id={"dp": lax.rem(target + nz, nz)}, device_id_type=MESH,
+            src_ref=src, dst_ref=rows(zs, place, c), send_sem=hop.at[len(hops)],
+            recv_sem=sem(kind, zs), device_id={"dp": lax.rem(target + nz, nz)}, device_id_type=MESH,
         )
         pl.when(inside)(copy.start)
         hops.append((inside, copy))
 
-    def rows(zs, place, core, part=None):
+    def rows(zs, place, core):
         start = zs * shard + (place * 2 + core) * piece
-        if part is None:
-            return basis.at[pl.ds(pl.multiple_of(start, piece), piece)]
-        return basis.at[pl.ds(pl.multiple_of(start + part * half, half), half)]
+        return basis.at[pl.ds(pl.multiple_of(start, piece), piece)]
 
     def sem(kind, zs):
         return arrive_basis.at[kind * nz + zs]
 
-    mine = basis_ref.at[pl.ds(pl.multiple_of((j * 2 + c) * piece, piece), piece)]
-    relay(0, mine, z, z + 1)
-    relay(1, mine, z, z - 1)
+    def start_own(place, kind):
+        mine = basis_ref.at[pl.ds(pl.multiple_of((place * 2 + c) * piece, piece), piece)]
+        relay(mine, z, place, kind, z + 1)
+        relay(mine, z, place, kind, z - 1)
+
+    start_own(j, FROM_Z)
     get_basis = pltpu.make_async_copy(
         basis_ref, basis.at[pl.ds(pl.multiple_of(z * shard, shard), shard)], local.at[0])
     get_act = pltpu.make_async_copy(
@@ -129,26 +129,14 @@
         s = jnp.where(k < near, k, k + 1)
         return jnp.where(z < nz // 2, s, nz - 1 - s)
 
-    def forward(zs):
-        arrived(rows(zs, a, c), sem(FROM_A, zs))
-        push(rows(zs, a, c, 0), rows(zs, a, c, 0), sem(HALF0_B, zs), to_b)
-        push(rows(zs, a, c), rows(zs, a, c), sem(SIB_A, zs), to_sib)
-        arrived(rows(zs, b, c), sem(FROM_B, zs))
-        push(rows(zs, b, c, 1), rows(zs, b, c, 1), sem(HALF1_A, zs), to_a)
-        push(rows(zs, b, c), rows(zs, b, c), sem(SIB_B, zs), to_sib)
-
-    def finish(zs):
-        arrived(rows(zs, opposite, c, 0), sem(HALF0_B, zs))
-        push(rows(zs, opposite, c, 0), rows(zs, opposite, c, 0), sem(SIB_H0, zs), to_sib)
-        arrived(rows(zs, opposite, c, 1), sem(HALF1_A, zs))
-        push(rows(zs, opposite, c, 1), rows(zs, opposite, c, 1), sem(SIB_H1, zs), to_sib)
+    def to_sibling(zs, place, kind):
+        push(rows(zs, place, c), rows(zs, place, c), sem(kind, zs), to_sib)
 
     def collect(zs):
         arrived(rows(zs, j, 1 - c), sem(SIB_OWN, zs))
         arrived(rows(zs, a, 1 - c), sem(SIB_A, zs))
         arrived(rows(zs, b, 1 - c), sem(SIB_B, zs))
-        arrived(rows(zs, opposite, 1 - c, 0), sem(SIB_H0, zs))
-        arrived(rows(zs, opposite, 1 - c, 1), sem(SIB_H1, zs))
+        arrived(rows(zs, opposite, 1 - c), sem(SIB_O, zs))
 
     depth = min(512, shard)
 
@@ -161,23 +149,33 @@
     for k in range(nz - 1):
         zs = source(k)
         arrived(rows(zs, j, c), sem(FROM_Z, zs))
-        relay(2 + k, rows(zs, j, c), zs, jnp.where(zs < z, z + 1, z - 1))
+        relay(rows(zs, j, c), zs, j, FROM_Z, jnp.where(zs < z, z + 1, z - 1))
         push(rows(zs, j, c), rows(zs, j, c), sem(FROM_A, zs), to_a)
         push(rows(zs, j, c), rows(zs, j, c), sem(FROM_B, zs), to_b)
-        push(rows(zs, j, c), rows(zs, j, c), sem(SIB_OWN, zs), to_sib)
-    for k in range(nz - 1):
-        forward(source(k))
+        to_sibling(zs, j, SIB_OWN)
+    start_own(opposite, FROM_Z2)
     send_weights(0)
     send_weights(1)
     get_basis.wait()
     get_act.wait()
     acc[...] = jnp.zeros_like(acc)
     accumulate(z)
-    finish(source(0))
-    for k in range(1, nz - 1):
-        finish(source(k))
-        collect(source(k - 1))
-        accumulate(source(k - 1))
+    for k in range(nz - 1):
+        zs = source(k)
+        if k == nz - 2:
+            forward_weights(0)
+            forward_weights(1)
+            send_weights(2)
+        arrived(rows(zs, a, c), sem(FROM_A, zs))
+        to_sibling(zs, a, SIB_A)
+        arrived(rows(zs, b, c), sem(FROM_B, zs))
+        to_sibling(zs, b, SIB_B)
+        arrived(rows(zs, opposite, c), sem(FROM_Z2, zs))
+        relay(rows(zs, opposite, c), zs, opposite, FROM_Z2, jnp.where(zs < z, z + 1, z - 1))
+        to_sibling(zs, opposite, SIB_O)
+        if k >= 1:
+            collect(source(k - 1))
+            accumulate(source(k - 1))
     collect(source(nz - 2))
     accumulate(source(nz - 2))
 
@@ -196,10 +194,8 @@
         arrived(low_rows(place, 1 - c), arrive_low.at[n])
     for n, place in enumerate((a, b, opposite)):
         arrived(grads.at[place], arrive_grads.at[n])
-    forward_weights(0)
-    forward_weights(1)
-    send_weights(2)
     send_weights(3)
+    forward_weights(2)
 
     def partial(peer):
         at = pl.ds(pl.multiple_of(peer * owned, owned), owned)
@@ -216,6 +212,7 @@
     for peer in peers:
         push(part_out.at[peer], part_in.at[z], arrive_part.at[z], {"dp": peer})
     part_own[...] = partial(z)
+    forward_weights(3)
 
     for peer in peers:
         arrived(part_in.at[peer], arrive_part.at[peer])
@@ -234,8 +231,6 @@
     for n, target in enumerate((to_a, to_b, to_o)):
         push(direction.at[j], direction.at[j], arrive_dir.at[n], target)
 
-    forward_weights(2)
-    forward_weights(3)
     for n, place in enumerate((a, b, opposite)):
         arrived(direction.at[place], arrive_dir.at[n])
     put_direction = pltpu.make_async_copy(direction, direction_out, local.at[5])
@@ -252,10 +247,14 @@
 
 
 def renew(direction_ref, basis_ref, weights_ref, out_ref):
-    update = lax.dot_general(
-        direction_ref[...], basis_ref[...], (((1,), (1,)), ((), ())), preferred_element_type=F32
-    )
-    out_ref[...] = (weights_ref[...].astype(F32) - step_scale * update).astype(BF16)
+    step = 256
+    for begin in range(0, out_ref.shape[1], step):
+        at = slice(begin, begin + step)
+        update = lax.dot_general(
+            direction_ref[...], basis_ref[at, :], (((1,), (1,)), ((), ())),
+            preferred_element_type=F32,
+        )
+        out_ref[:, at] = (weights_ref[:, at].astype(F32) - step_scale * update).astype(BF16)
 
 
 def shards(nz, activations, out_grads, basis, weights, first_moment, second_moment):
@@ -266,7 +265,7 @@
     vmem = pl.BlockSpec(memory_space=pltpu.VMEM)
     hbm = pl.BlockSpec(memory_space=pl.ANY)
     dma = pltpu.SemaphoreType.DMA
-    sends = (nz - 1) * 9 + (nz - 1) + 3 + 12 + 7 + 3
+    sends = (nz - 1) * 6 + (nz - 1) + 3 + 12 + 7 + 3
     gathered, weight_rows, direction, first_new, second_new = pl.pallas_call(
         functools.partial(kernel, nz),
         out_shape=(
@@ -293,9 +292,9 @@
             pltpu.VMEM((owned, rank), F32),
             pltpu.VMEM((owned, rank), F32),
             dma((8,)),
-            dma((nz + 1,)),
+            dma((2 * (nz + 1),)),
             dma((sends,)),
-            dma((10 * nz,)),
+            dma((8 * nz,)),
             dma((3,)),
             dma((7,)),
             dma((nz,)),

time: 185 us -> 173 us (0.935)
  Pallas kernels: 183 us -> 169 us
    pallas_call x1, Pallas kernels: 165 us -> 151 us  [shards(): pl.pallas_call(functools.partial(kernel, nz), out_shape=(jax.ShapeDtypeSt...]
where the time goes in v3:
time: 173 us; the launch traced here: 171 us
  Pallas kernels  169 us (98%)
    pallas_call x1, Pallas kernels, shards(): pl.pallas_call(functools.partial(kernel, nz), out_shape=(jax.ShapeDtypeSt...  151 us
    pallas_call x1, Pallas kernels, shards(): pl.pallas_call(renew, out_shape=jax.ShapeDtypeStruct((features, width), B...  17.7 us

profile of v3, /device:TPU:0, one launch (start us, length us, event | category | flops | bytes accessed | tf_op | source)
XLA Modules:
  0.0 171.3 jit_solution(14299392799626126876)
XLA Ops:
  0.6 151.3 %gather_and_step.1 = (bf16[8192,1024]{1,0:T(8,128)(2,1)}, bf16[4,128,8192]{2,1,0:T(8,128)(2,1)}, bf16[4,128,1024]{2,1,0:T(8,128)(2,1)}, f32[128,1024]{1,0:T(8,128)}, f32[128,1024]{1,0:T(8,128)}) custom-call(bf16[256,8192]{1,0:T(8,128)(2,1)} %act_ref.1, bf16[256,2048]{1,0:T(8,128)(2,1)} %bitcast.12, bf16[2048,1024]{1,0:T(8,128)(2,1)} %basis_ref.1, ...), custom_call_target="tpu_custom_call" | custom-call | tf_op jit(solution)/shard_map/gather_and_step/pallas_call | solution.py:269
  152.0 0.0 copy-start.1
  152.0 0.0 copy-start
  152.0 17.7 %renew.1 = bf16[512,8192]{1,0:T(8,128)(2,1)} custom-call(bf16[512,1024]{1,0:T(8,128)(2,1)} %bitcast.13, bf16[8192,1024]{1,0:T(8,128)(2,1)} %get-tuple-element.9.basis_ref, bf16[512,8192]{1,0:T(8,128)(2,1)} %bitcast.10), custom_call_target="tpu_custom_call" | custom-call | tf_op jit(solution)/shard_map/renew/pallas_call | solution.py:310
  169.7 0.0 copy-done.1
  169.7 0.8 copy.11
  170.5 0.0 copy-done
  170.5 0.8 copy.12
Async XLA Ops:
  152.0 17.7 %copy-start.1 = (f32[128,1024]{1,0:T(8,128)S(1)}, f32[128,1024]{1,0:T(8,128)}, u32[]{:S(2)}) copy-start(f32[128,1024]{1,0:T(8,128)} %get-tuple-element.11) | copy-start | bytes 1572868
  152.0 18.5 %copy-start = (f32[128,1024]{1,0:T(8,128)S(1)}, f32[128,1024]{1,0:T(8,128)}, u32[]{:S(2)}) copy-start(f32[128,1024]{1,0:T(8,128)} %get-tuple-element.12) | copy-start | bytes 1572868

commit v4 on v3

--- a/solution.py
+++ b/solution.py
@@ -22,8 +22,8 @@
 
 def kernel(
     nz, act_ref, grads_ref, basis_ref, weights_ref, first_ref, second_ref,
-    basis_out, weights_out, direction_out, first_out, second_out,
-    act, basis, raw, turned, grads, low, part_out, part_in, part_own, direction, acc, first, second,
+    basis_out, weights_out, direction, first_out, second_out,
+    act, basis, raw, turned, grads, low, part_out, part_in, part_own, acc, first, second,
     local, hop, send, arrive_basis, arrive_grads, arrive_low, arrive_part, arrive_dir, arrive_w,
 ):
     z, j, c = lax.axis_index("dp"), lax.axis_index("fsdp"), lax.axis_index("tensor")
@@ -179,82 +179,117 @@
     collect(source(nz - 2))
     accumulate(source(nz - 2))
 
-    def low_rows(place, core):
-        return low.at[place, pl.ds(pl.multiple_of(core * tokens, tokens), tokens)]
+    parts = 2
+    rank = basis.shape[1] // parts
+
+    def cols(p):
+        return pl.ds(p * rank, rank)
+
+    def low_rows(place, core, p):
+        return low.at[place, pl.ds(pl.multiple_of(core * tokens, tokens), tokens), cols(p)]
 
     low[j, pl.ds(pl.multiple_of(c * tokens, tokens), tokens), :] = acc[...].astype(BF16)
-    for n, target in enumerate((to_a, to_b, to_o, to_sib)):
-        push(low_rows(j, c), low_rows(j, c), arrive_low.at[n], target)
+    for p in range(parts):
+        for n, target in enumerate((to_a, to_b, to_o, to_sib)):
+            push(low_rows(j, c, p), low_rows(j, c, p), arrive_low.at[7 * p + n], target)
     put_basis = pltpu.make_async_copy(basis, basis_out, local.at[4])
     put_basis.start()
     for n, place in enumerate((a, b, opposite)):
-        arrived(low_rows(place, c), arrive_low.at[n])
-        push(low_rows(place, c), low_rows(place, c), arrive_low.at[4 + n], to_sib)
-    for n, place in ((3, j), (4, a), (5, b), (6, opposite)):
-        arrived(low_rows(place, 1 - c), arrive_low.at[n])
-    for n, place in enumerate((a, b, opposite)):
         arrived(grads.at[place], arrive_grads.at[n])
-    send_weights(3)
-    forward_weights(2)
-
-    def partial(peer):
+
+    def partial(peer, p):
         at = pl.ds(pl.multiple_of(peer * owned, owned), owned)
-        total = jnp.dot(grads[0, at, :], low[0], preferred_element_type=F32)
+        total = jnp.dot(grads[0, at, :], low[0, :, cols(p)], preferred_element_type=F32)
         for place in range(1, 4):
-            total += jnp.dot(grads[place, at, :], low[place], preferred_element_type=F32)
+            total += jnp.dot(grads[place, at, :], low[place, :, cols(p)], preferred_element_type=F32)
         return total
 
-    @pl.loop(1, nz)
-    def _(step):
-        peer = lax.rem(z + step, nz)
-        part_out[peer] = partial(peer).astype(BF16)
-
-    for peer in peers:
-        push(part_out.at[peer], part_in.at[z], arrive_part.at[z], {"dp": peer})
-    part_own[...] = partial(z)
-    forward_weights(3)
-
-    for peer in peers:
-        arrived(part_in.at[peer], arrive_part.at[peer])
-        part_own[...] += part_in[peer].astype(F32)
-
+    def part_ref(ref, peer, p):
+        return ref.at[peer, :, cols(p)]
+
+    for p in range(parts):
+        for n, place in enumerate((a, b, opposite)):
+            arrived(low_rows(place, c, p), arrive_low.at[7 * p + n])
+            push(low_rows(place, c, p), low_rows(place, c, p), arrive_low.at[7 * p + 4 + n], to_sib)
+        if p == 0:
+            send_weights(3)
+            forward_weights(2)
+        for n, place in ((3, j), (4, a), (5, b), (6, opposite)):
+            arrived(low_rows(place, 1 - c, p), arrive_low.at[7 * p + n])
+
+        @pl.loop(1, nz)
+        def _(step):
+            peer = lax.rem(z + step, nz)
+            part_out[peer, :, cols(p)] = partial(peer, p).astype(BF16)
+
+        for peer in peers:
+            push(part_ref(part_out, peer, p), part_ref(part_in, z, p), arrive_part.at[p * nz + z], {"dp": peer})
+        part_own[:, cols(p)] = partial(z, p)
     get_first.wait()
     get_second.wait()
-    projected = part_own[...]
-    first_new = beta_one * first[...] + (1.0 - beta_one) * projected
-    second_new = beta_two * second[...] + (1.0 - beta_two) * projected * projected
-    first_out[...] = first_new
-    second_out[...] = second_new
-    corrected = first_new / (1.0 - beta_one**STEP)
-    scaled = jnp.sqrt(second_new / (1.0 - beta_two**STEP)) + epsilon
-    direction[j] = (corrected / scaled).astype(BF16)
-    for n, target in enumerate((to_a, to_b, to_o)):
-        push(direction.at[j], direction.at[j], arrive_dir.at[n], target)
-
-    for n, place in enumerate((a, b, opposite)):
-        arrived(direction.at[place], arrive_dir.at[n])
-    put_direction = pltpu.make_async_copy(direction, direction_out, local.at[5])
-    put_direction.start()
+
+    for p in range(parts):
+        at = cols(p)
+        for peer in peers:
+            arrived(part_ref(part_in, peer, p), arrive_part.at[p * nz + peer])
+            part_own[:, at] += part_in[peer, :, at].astype(F32)
+        projected = part_own[:, at]
+        first_new = beta_one * first[:, at] + (1.0 - beta_one) * projected
+        second_new = beta_two * second[:, at] + (1.0 - beta_two) * projected * projected
+        first_out[:, at] = first_new
+        second_out[:, at] = second_new
+        corrected = first_new / (1.0 - beta_one**STEP)
+        scaled = jnp.sqrt(second_new / (1.0 - beta_two**STEP)) + epsilon
+        direction[j, :, at] = (corrected / scaled).astype(BF16)
+        for n, target in enumerate((to_a, to_b, to_o)):
+            push(direction.at[j, :, at], direction.at[j, :, at], arrive_dir.at[3 * p + n], target)
+        if p == 0:
+            forward_weights(3)
+    for p in range(parts):
+        for n, place in enumerate((a, b, opposite)):
+            arrived(direction.at[place, :, cols(p)], arrive_dir.at[3 * p + n])
     for n in range(4):
         finish_weights(n)
     get_weights.wait()
     put_basis.wait()
-    put_direction.wait()
     for copy in pending:
         copy.wait_send()
     for inside, copy in hops:
         pl.when(inside)(copy.wait_send)
 
 
-def renew(direction_ref, basis_ref, weights_ref, out_ref):
-    step = 256
-    for begin in range(0, out_ref.shape[1], step):
-        at = slice(begin, begin + step)
-        update = lax.dot_general(
-            direction_ref[...], basis_ref[at, :], (((1,), (1,)), ((), ())),
-            preferred_element_type=F32,
-        )
-        out_ref[:, at] = (weights_ref[:, at].astype(F32) - step_scale * update).astype(BF16)
+def renew(direction_ref, basis_ref, weights_ref, out_ref, tiles, ready, in_sems, out_sems):
+    slots, block = tiles.shape[:2]
+    steps = out_ref.shape[1] // block
+
+    def at(t):
+        return pl.ds(pl.multiple_of(t * block, block), block)
+
+    def get(t, slot):
+        return pltpu.make_async_copy(basis_ref.at[at(t)], tiles.at[slot], in_sems.at[slot])
+
+    def put(t, slot):
+        return pltpu.make_async_copy(ready.at[slot], out_ref.at[:, at(t)], out_sems.at[slot])
+
+    for slot in range(slots):
+        get(slot, slot).start()
+
+    @pl.loop(0, steps // slots)
+    def _(i):
+        for slot in range(slots):
+            t = slots * i + slot
+            get(t, slot).wait()
+            update = lax.dot_general(
+                direction_ref[...], tiles[slot], (((1,), (1,)), ((), ())), preferred_element_type=F32
+            )
+            renewed = (weights_ref[:, at(t)].astype(F32) - step_scale * update).astype(BF16)
+            pl.when(i > 0)(put(t, slot).wait)
+            ready[slot] = renewed
+            put(t, slot).start()
+            pl.when(t + slots < steps)(get(t + slots, slot).start)
+
+    for slot in range(slots):
+        put(slot, slot).wait()
 
 
 def shards(nz, activations, out_grads, basis, weights, first_moment, second_moment):
@@ -263,20 +298,21 @@
     owned = first_moment.shape[1]
     features = 4 * owned
     vmem = pl.BlockSpec(memory_space=pltpu.VMEM)
-    hbm = pl.BlockSpec(memory_space=pl.ANY)
+    hbm = pl.BlockSpec(memory_space=pltpu.HBM)
     dma = pltpu.SemaphoreType.DMA
-    sends = (nz - 1) * 6 + (nz - 1) + 3 + 12 + 7 + 3
+    parts = 2
+    sends = (nz - 1) * 6 + 3 + 12 + parts * (nz - 1 + 7 + 3)
     gathered, weight_rows, direction, first_new, second_new = pl.pallas_call(
         functools.partial(kernel, nz),
         out_shape=(
             jax.ShapeDtypeStruct((nz * shard, rank), BF16),
-            jax.ShapeDtypeStruct((4, owned, width), BF16),
-            jax.ShapeDtypeStruct((4, owned, rank), BF16),
+            pltpu.VMEM((4, owned, width), BF16),
+            pltpu.VMEM((4, owned, rank), BF16),
             jax.ShapeDtypeStruct((owned, rank), F32),
             jax.ShapeDtypeStruct((owned, rank), F32),
         ),
         in_specs=[hbm] * 6,
-        out_specs=(hbm, hbm, hbm, vmem, vmem),
+        out_specs=(hbm, vmem, vmem, vmem, vmem),
         scratch_shapes=[
             pltpu.VMEM((tokens // 2, width), BF16),
             pltpu.VMEM((nz * shard, rank), BF16),
@@ -287,7 +323,6 @@
             pltpu.VMEM((nz, owned, rank), BF16),
             pltpu.VMEM((nz, owned, rank), BF16),
             pltpu.VMEM((owned, rank), F32),
-            pltpu.VMEM((4, owned, rank), BF16),
             pltpu.VMEM((tokens // 2, rank), F32),
             pltpu.VMEM((owned, rank), F32),
             pltpu.VMEM((owned, rank), F32),
@@ -296,28 +331,29 @@
             dma((sends,)),
             dma((8 * nz,)),
             dma((3,)),
-            dma((7,)),
-            dma((nz,)),
-            dma((3,)),
+            dma((parts * 7,)),
+            dma((parts * nz,)),
+            dma((parts * 3,)),
             dma((12,)),
         ],
         compiler_params=pltpu.CompilerParams(
-            collective_id=0, has_side_effects=True, vmem_limit_bytes=60 * 2**20
+            collective_id=0, has_side_effects=True, vmem_limit_bytes=46 * 2**20
         ),
         name="gather_and_step",
     )(activations, out_grads[:, 0, :], basis, weights[0], first_moment[0], second_moment[0])
-    block = 1024
+    block = 512
     new_weights = pl.pallas_call(
         renew,
         out_shape=jax.ShapeDtypeStruct((features, width), BF16),
-        grid=(width // block,),
-        in_specs=[
-            pl.BlockSpec((features, rank), lambda i: (0, 0)),
-            pl.BlockSpec((block, rank), lambda i: (i, 0)),
-            pl.BlockSpec((features, block), lambda i: (0, i)),
+        in_specs=[vmem, hbm, vmem],
+        out_specs=hbm,
+        scratch_shapes=[
+            pltpu.VMEM((4, block, rank), BF16),
+            pltpu.VMEM((4, features, block), BF16),
+            dma((4,)),
+            dma((4,)),
         ],
-        out_specs=pl.BlockSpec((features, block), lambda i: (0, i)),
-        compiler_params=pltpu.CompilerParams(vmem_limit_bytes=60 * 2**20),
+        compiler_params=pltpu.CompilerParams(vmem_limit_bytes=46 * 2**20),
         name="renew",
     )(direction.reshape(features, rank), gathered, weight_rows.reshape(features, width))
     return (new_weights[None], first_new[None], second_new[None])

time: 173 us -> 177 us (1.023)
  the two profiles are of different devices: /device:TPU:0 before, /device:TPU:13 now
where the time goes in v4:
time: 177 us
  Pallas kernels  172 us (97%)
  local copies, waits for them, and re-layouts  4.81 us (3%)
    pallas_call x1, Pallas kernels, shards(): pl.pallas_call(functools.partial(kernel, nz), out_shape=(jax.ShapeDtypeSt...  154 us
    pallas_call x1, Pallas kernels, shards(): pl.pallas_call(renew, out_shape=jax.ShapeDtypeStruct((features, width), B...  18.2 us
    unnamed x8, local copies, waits for them, and re-layouts  4.81 us

profile of v4, /device:TPU:13, one launch (start us, length us, event | category | flops | bytes accessed | tf_op | source)
XLA Modules:
  0.0 177.3 jit_solution(13372690217650708787)
XLA Ops:
  0.6 153.6 %gather_and_step.1 = (bf16[8192,1024]{1,0:T(8,128)(2,1)}, bf16[4,128,8192]{2,1,0:T(8,128)(2,1)S(1)}, bf16[4,128,1024]{2,1,0:T(8,128)(2,1)S(1)}, f32[128,1024]{1,0:T(8,128)}, f32[128,1024]{1,0:T(8,128)}) custom-call(bf16[256,8192]{1,0:T(8,128)(2,1)} %act_ref.1, bf16[256,2048]{1,0:T(8,128)(2,1)} %bitcast.13, bf16[2048,1024]{1,0:T(8,128)(2,1)} %basis_ref.1, ...), custom_call_target="tpu_custom_call" | custom-call | tf_op jit(solution)/shard_map/gather_and_step/pallas_call | solution.py:305
  154.3 0.0 copy-start
  154.3 3.2 %copy-done = bf16[4,128,8192]{2,1,0:T(8,128)(2,1)} copy-done((bf16[4,128,8192]{2,1,0:T(8,128)(2,1)}, bf16[4,128,8192]{2,1,0:T(8,128)(2,1)S(1)}, u32[]{:S(2)}) %copy-start) | copy-done | bytes 8388632
  157.5 0.0 copy-start.2
  157.5 0.0 copy-start.1
  157.5 18.2 %renew.1 = bf16[512,8192]{1,0:T(8,128)(2,1)} custom-call(bf16[512,1024]{1,0:T(8,128)(2,1)S(1)} %bitcast.10, bf16[8192,1024]{1,0:T(8,128)(2,1)} %get-tuple-element.9.basis_ref, bf16[512,8192]{1,0:T(8,128)(2,1)} %bitcast.9), custom_call_target="tpu_custom_call" | custom-call | tf_op jit(solution)/shard_map/renew/pallas_call | solution.py:345
  175.7 0.0 copy-done.2
  175.7 0.8 copy.11
  176.5 0.0 copy-done.1
  176.5 0.8 copy.12
Async XLA Ops:
  154.3 3.2 %copy-start = (bf16[4,128,8192]{2,1,0:T(8,128)(2,1)}, bf16[4,128,8192]{2,1,0:T(8,128)(2,1)S(1)}, u32[]{:S(2)}) copy-start(bf16[4,128,8192]{2,1,0:T(8,128)(2,1)S(1)} %get-tuple-element.10) | copy-start | bytes 25165828
  157.5 18.2 %copy-start.2 = (f32[128,1024]{1,0:T(8,128)S(1)}, f32[128,1024]{1,0:T(8,128)}, u32[]{:S(2)}) copy-start(f32[128,1024]{1,0:T(8,128)} %get-tuple-element.11) | copy-start | bytes 1572868
  157.5 19.0 %copy-start.1 = (f32[128,1024]{1,0:T(8,128)S(1)}, f32[128,1024]{1,0:T(8,128)}, u32[]{:S(2)}) copy-start(f32[128,1024]{1,0:T(8,128)} %get-tuple-element.12) | copy-start | bytes 1572868

commit v5 on v4

--- a/solution.py
+++ b/solution.py
@@ -22,8 +22,8 @@
 
 def kernel(
     nz, act_ref, grads_ref, basis_ref, weights_ref, first_ref, second_ref,
-    basis_out, weights_out, direction, first_out, second_out,
-    act, basis, raw, turned, grads, low, part_out, part_in, part_own, acc, first, second,
+    basis_out, weights_out, direction_out, first_out, second_out,
+    act, basis, raw, turned, grads, low, part_out, part_in, part_own, sums, direction, acc, first, second,
     local, hop, send, arrive_basis, arrive_grads, arrive_low, arrive_part, arrive_dir, arrive_w,
 ):
     z, j, c = lax.axis_index("dp"), lax.axis_index("fsdp"), lax.axis_index("tensor")
@@ -166,13 +166,13 @@
             forward_weights(0)
             forward_weights(1)
             send_weights(2)
+        arrived(rows(zs, opposite, c), sem(FROM_Z2, zs))
+        relay(rows(zs, opposite, c), zs, opposite, FROM_Z2, jnp.where(zs < z, z + 1, z - 1))
+        to_sibling(zs, opposite, SIB_O)
         arrived(rows(zs, a, c), sem(FROM_A, zs))
         to_sibling(zs, a, SIB_A)
         arrived(rows(zs, b, c), sem(FROM_B, zs))
         to_sibling(zs, b, SIB_B)
-        arrived(rows(zs, opposite, c), sem(FROM_Z2, zs))
-        relay(rows(zs, opposite, c), zs, opposite, FROM_Z2, jnp.where(zs < z, z + 1, z - 1))
-        to_sibling(zs, opposite, SIB_O)
         if k >= 1:
             collect(source(k - 1))
             accumulate(source(k - 1))
@@ -189,42 +189,48 @@
         return low.at[place, pl.ds(pl.multiple_of(core * tokens, tokens), tokens), cols(p)]
 
     low[j, pl.ds(pl.multiple_of(c * tokens, tokens), tokens), :] = acc[...].astype(BF16)
-    for p in range(parts):
-        for n, target in enumerate((to_a, to_b, to_o, to_sib)):
-            push(low_rows(j, c, p), low_rows(j, c, p), arrive_low.at[7 * p + n], target)
+    def low_half(place, core, p, side):
+        at = pl.ds(p * rank + side * (rank // 2), rank // 2)
+        return low.at[place, pl.ds(pl.multiple_of(core * tokens, tokens), tokens), at]
+
+    for p in range(parts):
+        for n, target in enumerate((to_a, to_b, to_sib)):
+            push(low_rows(j, c, p), low_rows(j, c, p), arrive_low.at[9 * p + n], target)
     put_basis = pltpu.make_async_copy(basis, basis_out, local.at[4])
     put_basis.start()
     for n, place in enumerate((a, b, opposite)):
         arrived(grads.at[place], arrive_grads.at[n])
 
-    def partial(peer, p):
-        at = pl.ds(pl.multiple_of(peer * owned, owned), owned)
-        total = jnp.dot(grads[0, at, :], low[0, :, cols(p)], preferred_element_type=F32)
-        for place in range(1, 4):
-            total += jnp.dot(grads[place, at, :], low[place, :, cols(p)], preferred_element_type=F32)
-        return total
-
     def part_ref(ref, peer, p):
         return ref.at[peer, :, cols(p)]
 
     for p in range(parts):
-        for n, place in enumerate((a, b, opposite)):
-            arrived(low_rows(place, c, p), arrive_low.at[7 * p + n])
-            push(low_rows(place, c, p), low_rows(place, c, p), arrive_low.at[7 * p + 4 + n], to_sib)
+        for n, place, target in ((0, a, to_b), (1, b, to_a)):
+            arrived(low_rows(place, c, p), arrive_low.at[9 * p + n])
+            onward = low_half(place, c, p, n)
+            push(onward, onward, arrive_low.at[9 * p + 3 + n], target)
+            push(low_rows(place, c, p), low_rows(place, c, p), arrive_low.at[9 * p + 5 + n], to_sib)
         if p == 0:
             send_weights(3)
             forward_weights(2)
-        for n, place in ((3, j), (4, a), (5, b), (6, opposite)):
-            arrived(low_rows(place, 1 - c, p), arrive_low.at[7 * p + n])
-
-        @pl.loop(1, nz)
-        def _(step):
-            peer = lax.rem(z + step, nz)
-            part_out[peer, :, cols(p)] = partial(peer, p).astype(BF16)
+        for side in range(2):
+            corner = low_half(opposite, c, p, side)
+            arrived(corner, arrive_low.at[9 * p + 3 + side])
+            push(corner, corner, arrive_low.at[9 * p + 7 + side], to_sib)
+        for n, place in ((2, j), (5, a), (6, b)):
+            arrived(low_rows(place, 1 - c, p), arrive_low.at[9 * p + n])
+        for side in range(2):
+            arrived(low_half(opposite, 1 - c, p, side), arrive_low.at[9 * p + 7 + side])
+        total = jnp.dot(grads[0], low[0, :, cols(p)], preferred_element_type=F32)
+        for place in range(1, 4):
+            total += jnp.dot(grads[place], low[place, :, cols(p)], preferred_element_type=F32)
+        sums[...] = total
+        for zs in range(nz):
+            part_out[zs, :, cols(p)] = sums[zs * owned : (zs + 1) * owned, :].astype(BF16)
 
         for peer in peers:
             push(part_ref(part_out, peer, p), part_ref(part_in, z, p), arrive_part.at[p * nz + z], {"dp": peer})
-        part_own[:, cols(p)] = partial(z, p)
+        part_own[:, cols(p)] = sums[pl.ds(pl.multiple_of(z * owned, owned), owned), :]
     get_first.wait()
     get_second.wait()
 
@@ -241,55 +247,33 @@
         corrected = first_new / (1.0 - beta_one**STEP)
         scaled = jnp.sqrt(second_new / (1.0 - beta_two**STEP)) + epsilon
         direction[j, :, at] = (corrected / scaled).astype(BF16)
-        for n, target in enumerate((to_a, to_b, to_o)):
-            push(direction.at[j, :, at], direction.at[j, :, at], arrive_dir.at[3 * p + n], target)
+        for n, target in enumerate((to_a, to_b)):
+            push(direction.at[j, :, at], direction.at[j, :, at], arrive_dir.at[4 * p + n], target)
         if p == 0:
             forward_weights(3)
-    for p in range(parts):
-        for n, place in enumerate((a, b, opposite)):
-            arrived(direction.at[place, :, cols(p)], arrive_dir.at[3 * p + n])
+
+    def direction_half(place, p, side):
+        return direction.at[place, :, pl.ds(p * rank + side * (rank // 2), rank // 2)]
+
+    for p in range(parts):
+        for n, place, target in ((0, a, to_b), (1, b, to_a)):
+            arrived(direction.at[place, :, cols(p)], arrive_dir.at[4 * p + n])
+            onward = direction_half(place, p, n)
+            push(onward, onward, arrive_dir.at[4 * p + 2 + n], target)
+    for p in range(parts):
+        for side in range(2):
+            arrived(direction_half(opposite, p, side), arrive_dir.at[4 * p + 2 + side])
+    put_direction = pltpu.make_async_copy(direction, direction_out, local.at[5])
+    put_direction.start()
     for n in range(4):
         finish_weights(n)
     get_weights.wait()
     put_basis.wait()
+    put_direction.wait()
     for copy in pending:
         copy.wait_send()
     for inside, copy in hops:
         pl.when(inside)(copy.wait_send)
-
-
-def renew(direction_ref, basis_ref, weights_ref, out_ref, tiles, ready, in_sems, out_sems):
-    slots, block = tiles.shape[:2]
-    steps = out_ref.shape[1] // block
-
-    def at(t):
-        return pl.ds(pl.multiple_of(t * block, block), block)
-
-    def get(t, slot):
-        return pltpu.make_async_copy(basis_ref.at[at(t)], tiles.at[slot], in_sems.at[slot])
-
-    def put(t, slot):
-        return pltpu.make_async_copy(ready.at[slot], out_ref.at[:, at(t)], out_sems.at[slot])
-
-    for slot in range(slots):
-        get(slot, slot).start()
-
-    @pl.loop(0, steps // slots)
-    def _(i):
-        for slot in range(slots):
-            t = slots * i + slot
-            get(t, slot).wait()
-            update = lax.dot_general(
-                direction_ref[...], tiles[slot], (((1,), (1,)), ((), ())), preferred_element_type=F32
-            )
-            renewed = (weights_ref[:, at(t)].astype(F32) - step_scale * update).astype(BF16)
-            pl.when(i > 0)(put(t, slot).wait)
-            ready[slot] = renewed
-            put(t, slot).start()
-            pl.when(t + slots < steps)(get(t + slots, slot).start)
-
-    for slot in range(slots):
-        put(slot, slot).wait()
 
 
 def shards(nz, activations, out_grads, basis, weights, first_moment, second_moment):
@@ -301,18 +285,18 @@
     hbm = pl.BlockSpec(memory_space=pltpu.HBM)
     dma = pltpu.SemaphoreType.DMA
     parts = 2
-    sends = (nz - 1) * 6 + 3 + 12 + parts * (nz - 1 + 7 + 3)
+    sends = (nz - 1) * 6 + 3 + 12 + parts * (nz - 1 + 9 + 4)
     gathered, weight_rows, direction, first_new, second_new = pl.pallas_call(
         functools.partial(kernel, nz),
         out_shape=(
             jax.ShapeDtypeStruct((nz * shard, rank), BF16),
-            pltpu.VMEM((4, owned, width), BF16),
-            pltpu.VMEM((4, owned, rank), BF16),
+            jax.ShapeDtypeStruct((4, owned, width), BF16),
+            jax.ShapeDtypeStruct((4, owned, rank), BF16),
             jax.ShapeDtypeStruct((owned, rank), F32),
             jax.ShapeDtypeStruct((owned, rank), F32),
         ),
         in_specs=[hbm] * 6,
-        out_specs=(hbm, vmem, vmem, vmem, vmem),
+        out_specs=(hbm, hbm, hbm, vmem, vmem),
         scratch_shapes=[
             pltpu.VMEM((tokens // 2, width), BF16),
             pltpu.VMEM((nz * shard, rank), BF16),
@@ -323,6 +307,8 @@
             pltpu.VMEM((nz, owned, rank), BF16),
             pltpu.VMEM((nz, owned, rank), BF16),
             pltpu.VMEM((owned, rank), F32),
+            pltpu.VMEM((nz * owned, rank // parts), F32),
+            pltpu.VMEM((4, owned, rank), BF16),
             pltpu.VMEM((tokens // 2, rank), F32),
             pltpu.VMEM((owned, rank), F32),
             pltpu.VMEM((owned, rank), F32),
@@ -331,31 +317,22 @@
             dma((sends,)),
             dma((8 * nz,)),
             dma((3,)),
-            dma((parts * 7,)),
+            dma((parts * 9,)),
             dma((parts * nz,)),
-            dma((parts * 3,)),
+            dma((parts * 4,)),
             dma((12,)),
         ],
         compiler_params=pltpu.CompilerParams(
-            collective_id=0, has_side_effects=True, vmem_limit_bytes=46 * 2**20
+            collective_id=0, has_side_effects=True, vmem_limit_bytes=60 * 2**20
         ),
         name="gather_and_step",
     )(activations, out_grads[:, 0, :], basis, weights[0], first_moment[0], second_moment[0])
-    block = 512
-    new_weights = pl.pallas_call(
-        renew,
-        out_shape=jax.ShapeDtypeStruct((features, width), BF16),
-        in_specs=[vmem, hbm, vmem],
-        out_specs=hbm,
-        scratch_shapes=[
-            pltpu.VMEM((4, block, rank), BF16),
-            pltpu.VMEM((4, features, block), BF16),
-            dma((4,)),
-            dma((4,)),
-        ],
-        compiler_params=pltpu.CompilerParams(vmem_limit_bytes=46 * 2**20),
-        name="renew",
-    )(direction.reshape(features, rank), gathered, weight_rows.reshape(features, width))
+    update = lax.dot_general(
+        direction.reshape(features, rank), gathered, (((1,), (1,)), ((), ())),
+        preferred_element_type=F32,
+    )
+    rows = weight_rows.reshape(features, width)
+    new_weights = (rows.astype(F32) - step_scale * update).astype(BF16)
     return (new_weights[None], first_new[None], second_new[None])
 
 

time: 177 us -> 176 us (level)
  the two profiles are of different devices: /device:TPU:13 before, /device:TPU:0 now
where the time goes in v5:
time: 176 us; the launch traced here: 175 us
  Pallas kernels  157 us (89%)
  matrix products  16 us (9%)
    pallas_call x1, Pallas kernels, shards(): pl.pallas_call(functools.partial(kernel, nz), out_shape=(jax.ShapeDtypeSt...  157 us
    dot_general x1, matrix products, shards(): lax.dot_general(direction.reshape(features, rank), gathered, (((1,), (1,)...  16 us

profile of v5, /device:TPU:0, one launch (start us, length us, event | category | flops | bytes accessed | tf_op | source)
XLA Modules:
  0.0 175.4 jit_solution(9734655403292579969)
XLA Ops:
  0.6 157.1 %gather_and_step.1 = (bf16[8192,1024]{1,0:T(8,128)(2,1)}, bf16[4,128,8192]{2,1,0:T(8,128)(2,1)}, bf16[4,128,1024]{2,1,0:T(8,128)(2,1)}, f32[128,1024]{1,0:T(8,128)}, f32[128,1024]{1,0:T(8,128)}) custom-call(bf16[256,8192]{1,0:T(8,128)(2,1)} %act_ref.1, bf16[256,2048]{1,0:T(8,128)(2,1)} %bitcast.14, bf16[2048,1024]{1,0:T(8,128)(2,1)} %basis_ref.1, ...), custom_call_target="tpu_custom_call" | custom-call | tf_op jit(solution)/shard_map/gather_and_step/pallas_call | solution.py:289
  157.7 0.0 copy-start.1
  157.7 0.0 copy-start
  157.7 16.0 %fusion.1 = bf16[1,512,8192]{2,1,0:T(8,128)(2,1)} fusion(bf16[512,1024]{1,0:T(8,128)(2,1)} %bitcast.20, bf16[8192,1024]{1,0:T(8,128)(2,1)} %get-tuple-element.10, bf16[512,8192]{1,0:T(8,128)(2,1)} %bitcast.19), kind=kOutput, calls=%fused_computation.2 | convolution fusion | flops 8606711808 | bytes 34603008 | tf_op jit(solution)/shard_map/dot_general | solution.py:330
  173.8 0.0 copy-done.1
  173.8 0.8 copy.11
  174.6 0.0 copy-done
  174.6 0.8 copy.12
Async XLA Ops:
  157.7 16.0 %copy-start.1 = (f32[128,1024]{1,0:T(8,128)S(1)}, f32[128,1024]{1,0:T(8,128)}, u32[]{:S(2)}) copy-start(f32[128,1024]{1,0:T(8,128)} %get-tuple-element.11) | copy-start | bytes 1572868
  157.7 16.8 %copy-start = (f32[128,1024]{1,0:T(8,128)S(1)}, f32[128,1024]{1,0:T(8,128)}, u32[]{:S(2)}) copy-start(f32[128,1024]{1,0:T(8,128)} %get-tuple-element.12) | copy-start | bytes 1572868

commit v6 on v5

--- a/solution.py
+++ b/solution.py
@@ -162,10 +162,6 @@
     accumulate(z)
     for k in range(nz - 1):
         zs = source(k)
-        if k == nz - 2:
-            forward_weights(0)
-            forward_weights(1)
-            send_weights(2)
         arrived(rows(zs, opposite, c), sem(FROM_Z2, zs))
         relay(rows(zs, opposite, c), zs, opposite, FROM_Z2, jnp.where(zs < z, z + 1, z - 1))
         to_sibling(zs, opposite, SIB_O)
@@ -173,6 +169,9 @@
         to_sibling(zs, a, SIB_A)
         arrived(rows(zs, b, c), sem(FROM_B, zs))
         to_sibling(zs, b, SIB_B)
+        if k == nz - 2:
+            forward_weights(0)
+            forward_weights(1)
         if k >= 1:
             collect(source(k - 1))
             accumulate(source(k - 1))
@@ -189,13 +188,9 @@
         return low.at[place, pl.ds(pl.multiple_of(core * tokens, tokens), tokens), cols(p)]
 
     low[j, pl.ds(pl.multiple_of(c * tokens, tokens), tokens), :] = acc[...].astype(BF16)
-    def low_half(place, core, p, side):
-        at = pl.ds(p * rank + side * (rank // 2), rank // 2)
-        return low.at[place, pl.ds(pl.multiple_of(core * tokens, tokens), tokens), at]
-
     for p in range(parts):
-        for n, target in enumerate((to_a, to_b, to_sib)):
-            push(low_rows(j, c, p), low_rows(j, c, p), arrive_low.at[9 * p + n], target)
+        for n, target in enumerate((to_a, to_b, to_o, to_sib)):
+            push(low_rows(j, c, p), low_rows(j, c, p), arrive_low.at[7 * p + n], target)
     put_basis = pltpu.make_async_copy(basis, basis_out, local.at[4])
     put_basis.start()
     for n, place in enumerate((a, b, opposite)):
@@ -205,22 +200,14 @@
         return ref.at[peer, :, cols(p)]
 
     for p in range(parts):
-        for n, place, target in ((0, a, to_b), (1, b, to_a)):
-            arrived(low_rows(place, c, p), arrive_low.at[9 * p + n])
-            onward = low_half(place, c, p, n)
-            push(onward, onward, arrive_low.at[9 * p + 3 + n], target)
-            push(low_rows(place, c, p), low_rows(place, c, p), arrive_low.at[9 * p + 5 + n], to_sib)
+        for n, place in enumerate((a, b, opposite)):
+            arrived(low_rows(place, c, p), arrive_low.at[7 * p + n])
+            push(low_rows(place, c, p), low_rows(place, c, p), arrive_low.at[7 * p + 4 + n], to_sib)
         if p == 0:
+            send_weights(2)
             send_weights(3)
-            forward_weights(2)
-        for side in range(2):
-            corner = low_half(opposite, c, p, side)
-            arrived(corner, arrive_low.at[9 * p + 3 + side])
-            push(corner, corner, arrive_low.at[9 * p + 7 + side], to_sib)
-        for n, place in ((2, j), (5, a), (6, b)):
-            arrived(low_rows(place, 1 - c, p), arrive_low.at[9 * p + n])
-        for side in range(2):
-            arrived(low_half(opposite, 1 - c, p, side), arrive_low.at[9 * p + 7 + side])
+        for n, place in ((3, j), (4, a), (5, b), (6, opposite)):
+            arrived(low_rows(place, 1 - c, p), arrive_low.at[7 * p + n])
         total = jnp.dot(grads[0], low[0, :, cols(p)], preferred_element_type=F32)
         for place in range(1, 4):
             total += jnp.dot(grads[place], low[place, :, cols(p)], preferred_element_type=F32)
@@ -231,6 +218,7 @@
         for peer in peers:
             push(part_ref(part_out, peer, p), part_ref(part_in, z, p), arrive_part.at[p * nz + z], {"dp": peer})
         part_own[:, cols(p)] = sums[pl.ds(pl.multiple_of(z * owned, owned), owned), :]
+    forward_weights(2)
     get_first.wait()
     get_second.wait()
 
@@ -247,22 +235,12 @@
         corrected = first_new / (1.0 - beta_one**STEP)
         scaled = jnp.sqrt(second_new / (1.0 - beta_two**STEP)) + epsilon
         direction[j, :, at] = (corrected / scaled).astype(BF16)
-        for n, target in enumerate((to_a, to_b)):
-            push(direction.at[j, :, at], direction.at[j, :, at], arrive_dir.at[4 * p + n], target)
-        if p == 0:
-            forward_weights(3)
-
-    def direction_half(place, p, side):
-        return direction.at[place, :, pl.ds(p * rank + side * (rank // 2), rank // 2)]
-
+        for n, target in enumerate((to_a, to_b, to_o)):
+            push(direction.at[j, :, at], direction.at[j, :, at], arrive_dir.at[3 * p + n], target)
+    forward_weights(3)
     for p in range(parts):
-        for n, place, target in ((0, a, to_b), (1, b, to_a)):
-            arrived(direction.at[place, :, cols(p)], arrive_dir.at[4 * p + n])
-            onward = direction_half(place, p, n)
-            push(onward, onward, arrive_dir.at[4 * p + 2 + n], target)
-    for p in range(parts):
-        for side in range(2):
-            arrived(direction_half(opposite, p, side), arrive_dir.at[4 * p + 2 + side])
+        for n, place in enumerate((a, b, opposite)):
+            arrived(direction.at[place, :, cols(p)], arrive_dir.at[3 * p + n])
     put_direction = pltpu.make_async_copy(direction, direction_out, local.at[5])
     put_direction.start()
     for n in range(4):
@@ -285,7 +263,7 @@
     hbm = pl.BlockSpec(memory_space=pltpu.HBM)
     dma = pltpu.SemaphoreType.DMA
     parts = 2
-    sends = (nz - 1) * 6 + 3 + 12 + parts * (nz - 1 + 9 + 4)
+    sends = (nz - 1) * 6 + 3 + 12 + parts * (nz - 1 + 7 + 3)
     gathered, weight_rows, direction, first_new, second_new = pl.pallas_call(
         functools.partial(kernel, nz),
         out_shape=(
@@ -317,9 +295,9 @@
             dma((sends,)),
             dma((8 * nz,)),
             dma((3,)),
-            dma((parts * 9,)),
+            dma((parts * 7,)),
             dma((parts * nz,)),
-            dma((parts * 4,)),
+            dma((parts * 3,)),
             dma((12,)),
         ],
         compiler_params=pltpu.CompilerParams(

time: 176 us -> 166 us (0.943)
  Pallas kernels: 157 us -> 148 us
    pallas_call x1, Pallas kernels: 157 us -> 148 us  [shards(): pl.pallas_call(functools.partial(kernel, nz), out_shape=(jax.ShapeDtypeSt...]
where the time goes in v6:
time: 166 us
  Pallas kernels  148 us (89%)
  matrix products  16 us (10%)
    pallas_call x1, Pallas kernels, shards(): pl.pallas_call(functools.partial(kernel, nz), out_shape=(jax.ShapeDtypeSt...  148 us
    dot_general x1, matrix products, shards(): lax.dot_general(direction.reshape(features, rank), gathered, (((1,), (1,)...  16 us

profile of v6, /device:TPU:0, one launch (start us, length us, event | category | flops | bytes accessed | tf_op | source)
XLA Modules:
  0.0 166.1 jit_solution(16895308762234723502)
XLA Ops:
  0.6 147.8 %gather_and_step.1 = (bf16[8192,1024]{1,0:T(8,128)(2,1)}, bf16[4,128,8192]{2,1,0:T(8,128)(2,1)}, bf16[4,128,1024]{2,1,0:T(8,128)(2,1)}, f32[128,1024]{1,0:T(8,128)}, f32[128,1024]{1,0:T(8,128)}) custom-call(bf16[256,8192]{1,0:T(8,128)(2,1)} %act_ref.1, bf16[256,2048]{1,0:T(8,128)(2,1)} %bitcast.14, bf16[2048,1024]{1,0:T(8,128)(2,1)} %basis_ref.1, ...), custom_call_target="tpu_custom_call" | custom-call | tf_op jit(solution)/shard_map/gather_and_step/pallas_call | solution.py:267
  148.4 0.0 copy-start.1
  148.4 0.0 copy-start
  148.4 16.0 %fusion.1 = bf16[1,512,8192]{2,1,0:T(8,128)(2,1)} fusion(bf16[512,1024]{1,0:T(8,128)(2,1)} %bitcast.20, bf16[8192,1024]{1,0:T(8,128)(2,1)} %get-tuple-element.10, bf16[512,8192]{1,0:T(8,128)(2,1)} %bitcast.19), kind=kOutput, calls=%fused_computation.2 | convolution fusion | flops 8606711808 | bytes 34603008 | tf_op jit(solution)/shard_map/dot_general | solution.py:308
  164.5 0.0 copy-done.1
  164.5 0.8 copy.11
  165.3 0.0 copy-done
  165.3 0.8 copy.12
Async XLA Ops:
  148.4 16.0 %copy-start.1 = (f32[128,1024]{1,0:T(8,128)S(1)}, f32[128,1024]{1,0:T(8,128)}, u32[]{:S(2)}) copy-start(f32[128,1024]{1,0:T(8,128)} %get-tuple-element.11) | copy-start | bytes 1572868
  148.4 16.8 %copy-start = (f32[128,1024]{1,0:T(8,128)S(1)}, f32[128,1024]{1,0:T(8,128)}, u32[]{:S(2)}) copy-start(f32[128,1024]{1,0:T(8,128)} %get-tuple-element.12) | copy-start | bytes 1572868

commit v7 on v6

--- a/solution.py
+++ b/solution.py
@@ -178,7 +178,7 @@
     collect(source(nz - 2))
     accumulate(source(nz - 2))
 
-    parts = 2
+    parts = 4
     rank = basis.shape[1] // parts
 
     def cols(p):
@@ -262,7 +262,7 @@
     vmem = pl.BlockSpec(memory_space=pltpu.VMEM)
     hbm = pl.BlockSpec(memory_space=pltpu.HBM)
     dma = pltpu.SemaphoreType.DMA
-    parts = 2
+    parts = 4
     sends = (nz - 1) * 6 + 3 + 12 + parts * (nz - 1 + 7 + 3)
     gathered, weight_rows, direction, first_new, second_new = pl.pallas_call(
         functools.partial(kernel, nz),

time: 166 us -> 167 us (level)
  no operation moved by 1% of the time
where the time goes in v7:
time: 167 us
  Pallas kernels  148 us (89%)
  matrix products  16 us (10%)
    pallas_call x1, Pallas kernels, shards(): pl.pallas_call(functools.partial(kernel, nz), out_shape=(jax.ShapeDtypeSt...  148 us
    dot_general x1, matrix products, shards(): lax.dot_general(direction.reshape(features, rank), gathered, (((1,), (1,)...  16 us

profile of v7, /device:TPU:0, one launch (start us, length us, event | category | flops | bytes accessed | tf_op | source)
XLA Modules:
  0.0 166.6 jit_solution(13069466536398261215)
XLA Ops:
  0.6 148.3 %gather_and_step.1 = (bf16[8192,1024]{1,0:T(8,128)(2,1)}, bf16[4,128,8192]{2,1,0:T(8,128)(2,1)}, bf16[4,128,1024]{2,1,0:T(8,128)(2,1)}, f32[128,1024]{1,0:T(8,128)}, f32[128,1024]{1,0:T(8,128)}) custom-call(bf16[256,8192]{1,0:T(8,128)(2,1)} %act_ref.1, bf16[256,2048]{1,0:T(8,128)(2,1)} %bitcast.14, bf16[2048,1024]{1,0:T(8,128)(2,1)} %basis_ref.1, ...), custom_call_target="tpu_custom_call" | custom-call | tf_op jit(solution)/shard_map/gather_and_step/pallas_call | solution.py:267
  148.9 0.0 copy-start.1
  148.9 0.0 copy-start
  149.0 16.0 %fusion.1 = bf16[1,512,8192]{2,1,0:T(8,128)(2,1)} fusion(bf16[512,1024]{1,0:T(8,128)(2,1)} %bitcast.20, bf16[8192,1024]{1,0:T(8,128)(2,1)} %get-tuple-element.10, bf16[512,8192]{1,0:T(8,128)(2,1)} %bitcast.19), kind=kOutput, calls=%fused_computation.2 | convolution fusion | flops 8606711808 | bytes 34603008 | tf_op jit(solution)/shard_map/dot_general | solution.py:308
  165.0 0.0 copy-done.1
  165.0 0.8 copy.11
  165.8 0.0 copy-done
  165.8 0.8 copy.12
Async XLA Ops:
  148.9 16.0 %copy-start.1 = (f32[128,1024]{1,0:T(8,128)S(1)}, f32[128,1024]{1,0:T(8,128)}, u32[]{:S(2)}) copy-start(f32[128,1024]{1,0:T(8,128)} %get-tuple-element.11) | copy-start | bytes 1572868
  148.9 16.8 %copy-start = (f32[128,1024]{1,0:T(8,128)S(1)}, f32[128,1024]{1,0:T(8,128)}, u32[]{:S(2)}) copy-start(f32[128,1024]{1,0:T(8,128)} %get-tuple-element.12) | copy-start | bytes 1572868
